TPU v7x, 512 devices: a whole 4x4x16 slice. The times are simulated.
512 devices in a mesh: ctx: 64 (over z, x_hi, core), head: 8 (over y, x_lo).
Axes of the slice: x: 4 (x_hi: 2, x_lo: 2; x = x_hi * 2 + x_lo), y: 4, z: 16, core: 2. Of those that a mesh axis runs over, the one named last changes fastest.
Arguments:
- queries: bfloat16 [8192, 8192], P('ctx', 'head'), may hold values from -6 to 6
- q_gain: float32 [128], replicated, may hold values from 0.5 to 2.5
- k_gain: float32 [128], replicated, may hold values from 0.5 to 2.5
- attn_gate: float32 [1], replicated, may hold values from 0.3 to 1.5
- vision: bfloat16 [8192, 8192], P('ctx', 'head'), may hold values from -6 to 6
- key_projection_matrix: bfloat16 [8192, 1024], P('ctx', 'head'), may hold values from -0.0625 to 0.0625
- value_projection_matrix: bfloat16 [8192, 1024], P('ctx', 'head'), may hold values from -0.0625 to 0.0625
- image_start: int32 [24], replicated, may hold values from 1 to 8191, as said below
- slot_image: int32 [128], replicated, may hold values from 0 to 24, as said below
Outputs:
- attended: bfloat16 [8192, 8192], P('ctx', 'head')
Inputs may be any that keep to these rules, and one draw needn't show every extreme that they name: `image_start`: strictly increasing; the first image stands at position 1 and the last at 8191. `slot_image`: value 24 marks an empty slot. Each image has 3 to 4 tiles and some image exactly 4. Used slots are each device's lowest slots, and the numbers of used slots of two devices differ by at most one.
All inputs are finite; a program needn't handle non-finite values.
Results may differ from a plain program's by a relative error of at most 0.011.
Values may be sent and summed in bfloat16 or wider, within the bound.
No kernel may reach another device: no remote copies, remote signals or barrier semaphores. Data moves between devices by JAX's collectives and lax.ppermute only.
A program may use at most 64 MiB of HBM per device.

v0:
```python
import functools
import math

import jax
import jax.numpy as jnp
from jax import lax
from jax.experimental import pallas as pl
from jax.experimental.pallas import tpu as pltpu
from jax.sharding import PartitionSpec as P

EPS = 1e-05
PLANE = 4
VMEM_LIMIT = 16 * 1024 * 1024
SPREAD_LIMIT = 62 * 1024 * 1024
HIDE = -30000.0
STRIDE = 4
SOURCES = ((0, (0, 1, 2, 3)), (-1, (0, 1, 2, 3)), (1, (0, 1, 2, 3)), (2, (0, 1, 2, 3)))

FIRST = 3


def source_rank(plane_rank, step, turn):
    return lax.rem(plane_rank + step + STRIDE, STRIDE) + STRIDE * turn


def params(**more):
    return pltpu.CompilerParams(vmem_limit_bytes=VMEM_LIMIT, **more)


def vmem():
    return pl.BlockSpec(memory_space=pltpu.VMEM)


def smem():
    return pl.BlockSpec(memory_space=pltpu.SMEM)


def spread_kernel(x_ref, out_ref, pieces_ref, sems):
    members, peers, blocks, _, width = out_ref.shape
    copies = []
    for member in range(members):
        for block in range(blocks):
            first = (block * members + member) * width
            pieces_ref[member, block] = x_ref[:, first : first + width]
        for peer in range(peers):
            copies.append(
                pltpu.make_async_copy(
                    pieces_ref.at[member], out_ref.at[member, peer], sems.at[len(copies)]
                )
            )
            copies[-1].start()
    for copy in copies:
        copy.wait()


def order_of(member):
    return member, member ^ 2, member ^ 1, member ^ 3


def products(place_ref, x_ref, weight_refs, sources):
    depth = x_ref.shape[3]
    total = None
    for ref, (step, several) in zip(weight_refs, sources):
        for at in range(0, len(several), 2):
            both = [source_rank(place_ref[0], step, several[at + i]) for i in range(2)]
            part = jnp.dot(
                jnp.concatenate(
                    [
                        jnp.concatenate([x_ref[member, rank] for rank in both], axis=1)
                        for member in order_of(place_ref[1])
                    ],
                    axis=0,
                ),
                ref[at : at + 2].reshape(2 * depth, ref.shape[2]),
                preferred_element_type=jnp.float32,
            )
            total = part if total is None else total + part
    return total


def project_first_kernel(place_ref, x_ref, *refs):
    refs[-1][...] = products(place_ref, x_ref, refs[:-1], SOURCES[:FIRST])


def pack_products(total):
    head_dim = total.shape[1] // 2
    keys = total[:, :head_dim]
    high = keys.astype(jnp.bfloat16)
    low = (keys - high.astype(jnp.float32)).astype(jnp.bfloat16)
    return jnp.concatenate([high, low, total[:, head_dim:].astype(jnp.bfloat16)], axis=1)


def unpack_products(parts):
    head_dim = parts.shape[1] // 3
    parts = parts.astype(jnp.float32)
    keys = parts[:, :head_dim] + parts[:, head_dim : 2 * head_dim]
    return jnp.concatenate([keys, parts[:, 2 * head_dim :]], axis=1)


def project_last_kernel(place_ref, x_ref, *refs):
    weight_refs, first_ref, out_refs = refs[:-4], refs[-4], refs[-3:]
    total = first_ref[...] + products(place_ref, x_ref, weight_refs, SOURCES[FIRST:])
    packed = pack_products(total)
    rows = x_ref.shape[2]
    for out_ref, (start, stop) in zip(out_refs, ((0, 1), (1, 2), (2, 4))):
        out_ref[...] = packed[start * rows : stop * rows]


def add_products_kernel(kept_ref, came_ref, out_ref):
    rows = kept_ref.shape[0]
    out_ref[...] = pack_products(
        unpack_products(kept_ref[...]) + unpack_products(came_ref[rows:])
    )


def finish_kernel(kept_ref, core_ref, chip_ref, gain_ref, out_ref):
    rows = kept_ref.shape[0]
    raw = (
        unpack_products(kept_ref[...])
        + unpack_products(core_ref[:rows])
        + unpack_products(chip_ref[...])
    )
    head_dim = gain_ref.shape[1]
    keys = raw[:, :head_dim]
    mean = jnp.mean(keys * keys, axis=-1, keepdims=True)
    keys = keys * lax.rsqrt(mean + EPS) * gain_ref[...]
    out_ref[...] = jnp.concatenate([keys, raw[:, head_dim:]], axis=1).astype(out_ref.dtype)


def query_kernel(q_ref, gain_ref, out_ref):
    heads, _, head_dim = out_ref.shape
    for head in range(heads):
        raw = q_ref[:, head * head_dim : (head + 1) * head_dim].astype(jnp.float32)
        mean = jnp.mean(raw * raw, axis=-1, keepdims=True)
        out_ref[head] = (raw * lax.rsqrt(mean + EPS) * gain_ref[...]).astype(out_ref.dtype)


def split_sums(sums, heads):
    column = lax.broadcasted_iota(jnp.int32, sums.shape, 1)
    high = sums.astype(jnp.bfloat16).astype(jnp.float32)
    low = pltpu.roll(sums - high, heads, 1)
    return jnp.where(column < heads, high, jnp.where(column < 2 * heads, low, 0.0))


def join_sums(parts, heads):
    return parts + pltpu.roll(parts, parts.shape[1] - heads, 1)


def put_slot(keys_ref, values_ref, to, kv_ref, at, here, image):
    _, tile_rows, width = keys_ref.shape
    head_dim = width // 2
    rows = slice(here * tile_rows, (here + 1) * tile_rows)
    lane = lax.broadcasted_iota(jnp.int32, (tile_rows, head_dim), 1)
    mark = jnp.where(lane == image, HIDE, 0.0).astype(jnp.bfloat16)
    ones = jnp.ones((tile_rows, head_dim), jnp.bfloat16)
    keys_ref[to] = jnp.concatenate([kv_ref[at, rows, :head_dim], mark], axis=1)
    values_ref[to] = jnp.concatenate([kv_ref[at, rows, head_dim:], ones], axis=1)


def weigh(q_refs, halves, heads, several, late, keys, values, scale):
    q = [
        jnp.concatenate(
            [
                jnp.concatenate(
                    [ref[half * heads + head] for ref, half in zip(q_refs, halves)], axis=0
                ),
                late,
            ],
            axis=1,
        )
        for head in several
    ]
    scores = lax.dot_general(
        jnp.concatenate(q, axis=0),
        keys,
        (((1,), (1,)), ((), ())),
        preferred_element_type=jnp.float32,
    )
    weights = jnp.exp2(scores * scale).astype(jnp.bfloat16)
    total = jnp.dot(weights, values, preferred_element_type=jnp.float32)
    rows = late.shape[0]
    return [total[i * rows : (i + 1) * rows] for i in range(len(several))]


def attend_first_kernel(
    image_start_ref, slot_image_ref, place_ref, *refs, scale, slots_here, heads, halves
):
    kv_ref, q_refs = refs[0], refs[1 : 1 + PLANE]
    numer_ref, sums_ref, late_ref, keys_ref, values_ref = refs[1 + PLANE :]
    _, own, head_dim = q_refs[0].shape
    n_images = image_start_ref.shape[0]
    tokens = PLANE * own
    plane_rank = place_ref[0]
    member = place_ref[1]
    first_token = plane_rank * tokens
    total_tokens = tokens * (slot_image_ref.shape[0] // (slots_here * PLANE))

    lane = lax.broadcasted_iota(jnp.int32, (own, head_dim), 1)
    starts = jnp.full((own, head_dim), total_tokens, jnp.int32)
    for image in range(n_images):
        starts = jnp.where(lane == image, image_start_ref[image], starts)
    for at, one in enumerate(order_of(member)):
        position = (
            first_token + one * own + lax.broadcasted_iota(jnp.int32, (own, head_dim), 0)
        )
        late_ref[at * own : (at + 1) * own] = jnp.where(starts > position, 1.0, 0.0).astype(
            jnp.bfloat16
        )

    step, several = SOURCES[0]
    for at, turn in enumerate(several):
        rank = source_rank(plane_rank, step, turn)
        for here in range(slots_here):
            image = slot_image_ref[(rank * PLANE + member) * slots_here + here]
            put_slot(keys_ref, values_ref, at * slots_here + here, kv_ref, at, here, image)
    sums_ref[...] = jnp.zeros_like(sums_ref)
    column = lax.broadcasted_iota(jnp.int32, sums_ref.shape, 1)
    keys = keys_ref[...].reshape(-1, 2 * head_dim)
    values = values_ref[...].reshape(-1, 2 * head_dim)
    together = 2

    def some_heads(number, _):
        several = [number * together + i for i in range(together)]
        totals = weigh(q_refs, halves, heads, several, late_ref[...], keys, values, scale)
        sums = sums_ref[...]
        for head, total in zip(several, totals):
            at = pl.ds(pl.multiple_of(head * head_dim, head_dim), head_dim)
            numer_ref[:, at] = total[:, :head_dim].astype(numer_ref.dtype)
            sums = jnp.where(column == head, total[:, head_dim:], sums)
        sums_ref[...] = sums
        return 0

    lax.fori_loop(0, heads // together, some_heads, 0, unroll=2)


def attend_last_kernel(
    image_start_ref, slot_image_ref, place_ref, *refs, scale, group, slots_here, heads, halves
):
    sources = SOURCES[1:]
    kv_refs, q_refs = refs[: len(sources)], refs[len(sources) : len(sources) + PLANE]
    numer_ref, came_ref, late_ref, kept_ref, to_core_ref = refs[len(sources) + PLANE : -3]
    keys_ref, values_ref, sums_ref = refs[-3:]
    _, own, head_dim = q_refs[0].shape
    n_images = image_start_ref.shape[0]
    plane_rank = place_ref[0]
    limit = (plane_rank + 1) * PLANE * own

    put = functools.partial(put_slot, keys_ref, values_ref)
    kept = jnp.int32(0)
    for kv_ref, (step, several) in zip(kv_refs, sources):
        for at, turn in enumerate(several):
            rank = source_rank(plane_rank, step, turn)
            for here in range(slots_here):
                image = slot_image_ref[(rank * PLANE + place_ref[1]) * slots_here + here]
                start = image_start_ref[jnp.minimum(image, n_images - 1)]
                seen = jnp.logical_and(image < n_images, start < limit)
                pl.when(seen)(functools.partial(put, kept, kv_ref, at, here, image))
                kept = kept + seen.astype(jnp.int32)
    turns = (kept + group - 1) // group

    def fill(to, _):
        put(to, kv_refs[0], 0, 0, n_images)
        return 0

    lax.fori_loop(kept, turns * group, fill, 0)
    sums_ref[...] = came_ref[...]
    column = lax.broadcasted_iota(jnp.int32, sums_ref.shape, 1)
    half = 2 * own

    def one_head(head, _, count):
        keys = keys_ref[:count].reshape(-1, 2 * head_dim)
        values = values_ref[:count].reshape(-1, 2 * head_dim)
        [total] = weigh(q_refs, halves, heads, [head], late_ref[...], keys, values, scale)
        at = pl.ds(pl.multiple_of(head * head_dim, head_dim), head_dim)
        numer = (numer_ref[:, at].astype(jnp.float32) + total[:, :head_dim]).astype(jnp.bfloat16)
        kept_ref[:, at] = numer[:half]
        to_core_ref[:, at] = numer[half:]
        sums = sums_ref[...]
        sums_ref[...] = jnp.where(column == head, sums + total[:, head_dim:], sums)
        return 0

    for turn in range(1, keys_ref.shape[0] // group + 1):

        @pl.when(turns == turn)
        def _():
            lax.fori_loop(
                0, heads, functools.partial(one_head, count=turn * group), 0, unroll=2
            )

    @pl.when(turns == 0)
    def _():
        kept_ref[:, : heads * head_dim] = numer_ref[:half]
        to_core_ref[:, : heads * head_dim] = numer_ref[half:]

    sums = split_sums(sums_ref[...], heads).astype(jnp.bfloat16)
    kept_ref[:, heads * head_dim :] = sums[:half]
    to_core_ref[:, heads * head_dim :] = sums[half:]


def add_kernel(kept_ref, came_ref, out_ref, *, heads):
    own, width = out_ref.shape
    cut = width - 128
    for first in range(0, cut, 256):
        columns = slice(first, min(first + 256, cut))
        out_ref[:, columns] = (
            kept_ref[own:, columns].astype(jnp.float32)
            + came_ref[own:, columns].astype(jnp.float32)
        ).astype(out_ref.dtype)
    sums = kept_ref[own:, cut:].astype(jnp.float32) + came_ref[own:, cut:].astype(jnp.float32)
    out_ref[:, cut:] = split_sums(join_sums(sums, heads), heads).astype(out_ref.dtype)


def combine_kernel(image_start_ref, place_ref, gate_ref, kept_ref, core_ref, chip_ref, out_ref):
    own, out_width = out_ref.shape
    width = kept_ref.shape[1]
    head_dim = width - out_width
    heads = out_width // head_dim
    first = (place_ref[0] * PLANE + place_ref[1]) * own
    position = first + lax.broadcasted_iota(jnp.int32, (own, 1), 0)
    seen = position >= image_start_ref[0]
    factor = jnp.tanh(gate_ref[...])

    def total(columns):
        return (
            kept_ref[:own, columns].astype(jnp.float32)
            + core_ref[:own, columns].astype(jnp.float32)
            + chip_ref[:, columns].astype(jnp.float32)
        )

    sums = join_sums(total(slice(out_width, width)), heads)
    share = jnp.where(seen, factor / jnp.where(seen, sums, 1.0), 0.0)
    for head in range(heads):
        columns = slice(head * head_dim, (head + 1) * head_dim)
        out_ref[:, columns] = (total(columns) * share[:, head : head + 1]).astype(out_ref.dtype)


def gather_along_z(block, beside=None):
    ctx_size = lax.axis_size("ctx")
    ranks = ctx_size // PLANE

    def shift(value, *distances):
        moves = [distances[i % len(distances)] * PLANE for i in range(ctx_size)]
        return lax.ppermute(
            value, "ctx", [(i, (i + moves[i]) % ctx_size) for i in range(ctx_size)]
        )

    groups = [
        [rank * PLANE + member for rank in range(first, ranks, STRIDE)]
        for member in range(PLANE)
        for first in range(STRIDE)
    ]
    own = lax.all_gather(block, "ctx", axis_index_groups=groups)
    if beside is not None:
        own, beside = lax.optimization_barrier((own, beside))
    return (own, shift(own, 1), shift(own, -1), shift(own, 2, -2)), beside


def other_member(value, mask):
    ctx_size = lax.axis_size("ctx")
    return lax.ppermute(value, "ctx", [(i, i ^ mask) for i in range(ctx_size)])


def local(
    queries,
    q_gain,
    k_gain,
    attn_gate,
    vision,
    key_projection_matrix,
    value_projection_matrix,
    image_start,
    slot_image,
):
    ctx_size = lax.axis_size("ctx")
    head_size = lax.axis_size("head")
    ranks = ctx_size // PLANE
    own_index = lax.axis_index("ctx")
    plane_rank = own_index // PLANE
    member = own_index % PLANE
    place = jnp.stack([plane_rank, member]).astype(jnp.int32)
    head_dim = q_gain.shape[0]
    tokens, q_cols = queries.shape
    heads = q_cols // head_dim
    rows, features = vision.shape
    piece_rows, kv_cols = key_projection_matrix.shape
    in_plane = [[rank * PLANE + m for m in range(PLANE)] for rank in range(ranks)]
    whole_plane = [
        [rank * PLANE * head_size + i for i in range(PLANE * head_size)] for rank in range(ranks)
    ]

    with jax.named_scope("norm_queries"):
        normed = pl.pallas_call(
            query_kernel,
            out_shape=jax.ShapeDtypeStruct((heads, tokens, head_dim), jnp.bfloat16),
            in_specs=[vmem(), vmem()],
            out_specs=vmem(),
            compiler_params=params(),
        )(queries, q_gain.reshape(1, head_dim))

    with jax.named_scope("spread_vision"):
        blocks = features // (piece_rows * PLANE)
        mine = pl.pallas_call(
            spread_kernel,
            out_shape=jax.ShapeDtypeStruct(
                (PLANE, head_size, blocks, rows, piece_rows), jnp.bfloat16
            ),
            in_specs=[vmem()],
            out_specs=pl.BlockSpec(memory_space=pltpu.HBM),
            scratch_shapes=[
                pltpu.VMEM((PLANE, blocks, rows, piece_rows), jnp.bfloat16),
                pltpu.SemaphoreType.DMA((PLANE * head_size,)),
            ],
            compiler_params=pltpu.CompilerParams(vmem_limit_bytes=SPREAD_LIMIT),
        )(vision)
        mine = mine.reshape(PLANE * head_size, blocks, rows, piece_rows)
        spread = lax.all_to_all(mine, ("ctx", "head"), 0, 0, axis_index_groups=whole_plane)
        spread = spread.reshape(PLANE, ranks, rows, piece_rows)

    with jax.named_scope("gather_projections"):
        weights, _ = gather_along_z(
            jnp.concatenate([key_projection_matrix, value_projection_matrix], axis=1)
        )

    with jax.named_scope("share_queries"):
        core_queries = other_member(normed, 1)
        spread, core_queries = lax.optimization_barrier((spread, core_queries))
        chip_queries = other_member(jnp.concatenate([normed, core_queries]), 2)

    with jax.named_scope("project"):
        partial = pl.pallas_call(
            project_first_kernel,
            out_shape=jax.ShapeDtypeStruct((PLANE * rows, 2 * kv_cols), jnp.float32),
            in_specs=[smem()] + [vmem()] * (1 + FIRST),
            out_specs=vmem(),
            compiler_params=params(),
        )(place, spread, *weights[:FIRST])
        triple = 3 * kv_cols
        shapes = [(rows, triple), (rows, triple), (2 * rows, triple)]
        kept, to_chip, to_core = pl.pallas_call(
            project_last_kernel,
            out_shape=[jax.ShapeDtypeStruct(shape, jnp.bfloat16) for shape in shapes],
            in_specs=[smem()] + [vmem()] * (2 + len(weights) - FIRST),
            out_specs=[vmem()] * 3,
            compiler_params=params(),
        )(place, spread, *weights[FIRST:], partial)

    with jax.named_scope("sum_projections"):
        from_core = other_member(to_core, 1)
        to_chip = pl.pallas_call(
            add_products_kernel,
            out_shape=jax.ShapeDtypeStruct((rows, triple), jnp.bfloat16),
            in_specs=[vmem()] * 2,
            out_specs=vmem(),
            compiler_params=params(),
        )(to_chip, from_core)
        from_chip = other_member(to_chip, 2)
        own_kv = pl.pallas_call(
            finish_kernel,
            out_shape=jax.ShapeDtypeStruct((rows, 2 * kv_cols), jnp.bfloat16),
            in_specs=[vmem()] * 4,
            out_specs=vmem(),
            compiler_params=params(),
        )(kept, from_core, from_chip, k_gain.reshape(1, head_dim))

    with jax.named_scope("gather_keys_values"):
        all_kv, chip_queries = gather_along_z(own_kv, chip_queries)

    with jax.named_scope("attend"):
        slots_here = slot_image.shape[0] // ctx_size
        tile_rows = rows // slots_here
        slots = slots_here * len(SOURCES[0][1])
        last_slots = ranks * slots_here - slots
        group = math.gcd(last_slots, 4)
        width = q_cols + head_dim
        scale = head_dim ** (-0.5) * math.log2(math.e)
        plane_queries = [(normed, 0), (chip_queries, 0), (core_queries, 0), (chip_queries, 1)]

        def cost(rows_here, slots):
            scores = heads * rows_here * slots * tile_rows
            return pl.CostEstimate(
                flops=8 * scores * head_dim,
                bytes_accessed=4 * rows_here * width,
                transcendentals=scores,
            )

        numer, sums, late = pl.pallas_call(
            functools.partial(
                attend_first_kernel,
                scale=scale,
                slots_here=slots_here,
                heads=heads,
                halves=tuple(half for _, half in plane_queries),
            ),
            out_shape=[
                jax.ShapeDtypeStruct((PLANE * tokens, q_cols), jnp.bfloat16),
                jax.ShapeDtypeStruct((PLANE * tokens, head_dim), jnp.float32),
                jax.ShapeDtypeStruct((PLANE * tokens, head_dim), jnp.bfloat16),
            ],
            in_specs=[smem()] * 3 + [vmem()] * (1 + PLANE),
            out_specs=[vmem()] * 3,
            scratch_shapes=[pltpu.VMEM((slots, tile_rows, 2 * head_dim), jnp.bfloat16)] * 2,
            compiler_params=params(),
            cost_estimate=cost(PLANE * tokens, slots),
        )(
            image_start,
            slot_image,
            place,
            all_kv[0],
            *(source for source, _ in plane_queries),
        )
        own_and_chip, to_core = pl.pallas_call(
            functools.partial(
                attend_last_kernel,
                scale=scale,
                group=group,
                slots_here=slots_here,
                heads=heads,
                halves=tuple(half for _, half in plane_queries),
            ),
            out_shape=[jax.ShapeDtypeStruct((2 * tokens, width), jnp.bfloat16)] * 2,
            in_specs=[smem()] * 3 + [vmem()] * (len(all_kv) - 1 + PLANE + 3),
            out_specs=[vmem()] * 2,
            scratch_shapes=[
                pltpu.VMEM((last_slots, tile_rows, 2 * head_dim), jnp.bfloat16),
                pltpu.VMEM((last_slots, tile_rows, 2 * head_dim), jnp.bfloat16),
                pltpu.VMEM((PLANE * tokens, head_dim), jnp.float32),
            ],
            compiler_params=params(),
            cost_estimate=cost(PLANE * tokens, last_slots),
        )(
            image_start,
            slot_image,
            place,
            *all_kv[1:],
            *(source for source, _ in plane_queries),
            numer,
            sums,
            late,
        )
        from_core = other_member(to_core, 1)

    with jax.named_scope("sum_attention"):
        to_chip = pl.pallas_call(
            functools.partial(add_kernel, heads=heads),
            out_shape=jax.ShapeDtypeStruct((tokens, width), jnp.bfloat16),
            in_specs=[vmem(), vmem()],
            out_specs=vmem(),
            compiler_params=params(),
        )(own_and_chip, from_core)
        from_chip = other_member(to_chip, 2)
        return pl.pallas_call(
            combine_kernel,
            out_shape=jax.ShapeDtypeStruct((tokens, q_cols), jnp.bfloat16),
            in_specs=[smem(), smem()] + [vmem()] * 4,
            out_specs=vmem(),
            compiler_params=params(),
        )(image_start, place, attn_gate.reshape(1, 1), own_and_chip, from_core, from_chip)


def solution(mesh):
    in_specs = (
        P("ctx", "head"),
        P(),
        P(),
        P(),
        P("ctx", "head"),
        P("ctx", "head"),
        P("ctx", "head"),
        P(),
        P(),
    )
    out_specs = P("ctx", "head")
    return jax.shard_map(local, mesh=mesh, in_specs=in_specs, out_specs=out_specs, check_vma=False)
```

profile of v0, /device:TPU:1, one launch (start us, length us, event | category | flops | bytes accessed | tf_op | source)
XLA Modules:
  0.0 135.3 jit_solution(15221519956523452813)
XLA Ops:
  0.0 2.6 %spread_vision.1 = bf16[4,8,2,128,128]{4,3,2,1,0:T(8,128)(2,1)} custom-call(bf16[128,1024]{1,0:T(8,128)(2,1)} %x_ref.1), custom_call_target="tpu_custom_call" | custom-call | tf_op jit(solution)/shard_map/spread_vision/pallas_call | solution.py:402
  2.6 0.0 copy-start
  2.6 0.0 copy-start.1
  2.6 0.0 copy-start.5
  2.6 0.0 copy-start.6
  2.6 10.7 %all-to-all-start = ((bf16[32,2,128,128]{3,2,1,0:T(8,128)(2,1)}), bf16[32,2,128,128]{3,2,1,0:T(8,128)(2,1)S(1)}, u32[]{:S(2)}, u32[]{:S(2)}) async-start(bf16[32,2,128,128]{3,2,1,0:T(8,128)(2,1)} %bitcast.22), calls=%async_computation | async-start | bytes 4194304 | tf_op jit(solution)/shard_map/spread_vision/all_to_all | solution.py:416
  13.4 0.2 norm_queries.1.refs_1_.refs_3_
  13.6 2.2 %collective-permute-start = (bf16[8,128,128]{2,1,0:T(8,128)(2,1)S(1)}, bf16[8,128,128]{2,1,0:T(8,128)(2,1)}, u32[]{:S(2)}, u32[]{:S(2)}) collective-permute-start(bf16[8,128,128]{2,1,0:T(8,128)(2,1)S(1)} %norm_queries.1.refs_1_.refs_3_), channel_id=1, source_target_pairs={{0,8},{8,0},{16,24},{24,16},{32,40},{40,32},{48,56},{56,48},{64,72... | collective-permute-start | bytes 786440 | tf_op jit(solution)/shard_map/share_queries/ppermute | solution.py:360
  15.9 22.8 %all-gather = bf16[512,256]{1,0:T(8,128)(2,1)S(1)} all-gather(bf16[128,256]{1,0:T(8,128)(2,1)S(1)} %pad_maximum_fusion.1), channel_id=2, replica_groups={{0,128,256,384},{32,160,288,416},{64,192,320,448},{96,224,352,480},{8,1..., dimensions={0}, use_global_device_ids=true | all-gather | bytes 327680 | tf_op jit(solution)/shard_map/gather_projections/all_gather | solution.py:352
  38.7 2.7 %collective-permute-start.2 = (bf16[4,128,256]{2,1,0:T(8,128)(2,1)S(1)}, bf16[4,128,256]{2,1,0:T(8,128)(2,1)S(1)}, u32[]{:S(2)}, u32[]{:S(2)}) collective-permute-start(bf16[4,128,256]{2,1,0:T(8,128)(2,1)S(1)} %bitcast.12), channel_id=1, source_target_pairs={{0,32},{8,40},{16,48},{24,56},{32,64},{40,72},{48,80},{56,88},{64,... | collective-permute-start | bytes 786440 | tf_op jit(solution)/shard_map/gather_projections/ppermute | solution.py:343
  41.3 3.8 %collective-permute-start.3 = (bf16[4,128,256]{2,1,0:T(8,128)(2,1)S(1)}, bf16[4,128,256]{2,1,0:T(8,128)(2,1)S(1)}, u32[]{:S(2)}, u32[]{:S(2)}) collective-permute-start(bf16[4,128,256]{2,1,0:T(8,128)(2,1)S(1)} %bitcast.13), channel_id=1, source_target_pairs={{0,480},{8,488},{16,496},{24,504},{32,0},{40,8},{48,16},{56,24},{6... | collective-permute-start | bytes 786440 | tf_op jit(solution)/shard_map/gather_projections/ppermute | solution.py:343
  45.2 1.9 %collective-permute-start.1 = (bf16[4,128,256]{2,1,0:T(8,128)(2,1)S(1)}, bf16[4,128,256]{2,1,0:T(8,128)(2,1)S(1)}, u32[]{:S(2)}, u32[]{:S(2)}) collective-permute-start(bf16[4,128,256]{2,1,0:T(8,128)(2,1)S(1)} %bitcast.14), channel_id=1, source_target_pairs={{0,64},{8,456},{16,80},{24,472},{32,96},{40,488},{48,112},{56,504}... | collective-permute-start | bytes 786440 | tf_op jit(solution)/shard_map/gather_projections/ppermute | solution.py:343
  47.1 0.0 collective-permute-done.refs_3_.refs_5_
  47.1 0.0 all-to-all-done
  47.1 1.8 %pad_maximum_fusion = bf16[16,128,128]{2,1,0:T(8,128)(2,1)} fusion(bf16[8,128,128]{2,1,0:T(8,128)(2,1)} %collective-permute-done.refs_3_.refs_5_, bf16[8,128,128]{2,1,0:T(8,128)(2,1)S(1)} %norm_queries.1.refs_1_.refs_3_), kind=kLoop, calls=%fused_computation | loop fusion | flops 262144 | bytes 1048576 | tf_op jit(solution)/shard_map/share_queries/concatenate | solution.py:427
  48.9 4.7 %collective-permute-start.6 = (bf16[16,128,128]{2,1,0:T(8,128)(2,1)}, bf16[16,128,128]{2,1,0:T(8,128)(2,1)}, u32[]{:S(2)}, u32[]{:S(2)}) collective-permute-start(bf16[16,128,128]{2,1,0:T(8,128)(2,1)} %pad_maximum_fusion), channel_id=1, source_target_pairs={{0,16},{8,24},{16,0},{24,8},{32,48},{40,56},{48,32},{56,40},{64,80... | collective-permute-start | bytes 1572872 | tf_op jit(solution)/shard_map/share_queries/ppermute | solution.py:360
  53.6 0.1 pad_add_fusion.place_ref
  53.7 0.0 collective-permute-done.2.refs_1_
  53.7 0.0 collective-permute-done.3.refs_2_
  53.7 1.1 project.2.refs_1_
  54.8 0.0 copy-start.3
  54.8 0.0 copy-start.2
  54.8 0.0 copy-start.4
  54.8 3.5 %collective-permute-done.1.refs_0_ = bf16[4,128,256]{2,1,0:T(8,128)(2,1)S(1)} collective-permute-done((bf16[4,128,256]{2,1,0:T(8,128)(2,1)S(1)}, bf16[4,128,256]{2,1,0:T(8,128)(2,1)S(1)}, u32[]{:S(2)}, u32[]{:S(2)}) %collective-permute-start.1) | collective-permute-done | bytes 262176 | tf_op jit(solution)/shard_map/gather_projections/ppermute | solution.py:343
  58.4 0.8 project.3
  59.2 4.9 %collective-permute-start.4 = (bf16[256,384]{1,0:T(8,128)(2,1)S(1)}, bf16[256,384]{1,0:T(8,128)(2,1)S(1)}, u32[]{:S(2)}, u32[]{:S(2)}) collective-permute-start(bf16[256,384]{1,0:T(8,128)(2,1)S(1)} %get-tuple-element.19), channel_id=1, source_target_pairs={{0,8},{8,0},{16,24},{24,16},{32,40},{40,32},{48,56},{56,48},{64,72... | collective-permute-start | bytes 589832 | tf_op jit(solution)/shard_map/sum_projections/ppermute | solution.py:360
  64.1 1.0 collective-permute-done.4.came_ref.core_ref
  65.2 5.0 %collective-permute-start.5 = (bf16[128,384]{1,0:T(8,128)(2,1)S(1)}, bf16[128,384]{1,0:T(8,128)(2,1)S(1)}, u32[]{:S(2)}, u32[]{:S(2)}) collective-permute-start(bf16[128,384]{1,0:T(8,128)(2,1)S(1)} %sum_projections.2), channel_id=1, source_target_pairs={{0,16},{8,24},{16,0},{24,8},{32,48},{40,56},{48,32},{56,40},{64,80... | collective-permute-start | bytes 294920 | tf_op jit(solution)/shard_map/sum_projections/ppermute | solution.py:360
  70.2 2.7 %collective-permute-done.5.chip_ref = bf16[128,384]{1,0:T(8,128)(2,1)S(1)} collective-permute-done((bf16[128,384]{1,0:T(8,128)(2,1)S(1)}, bf16[128,384]{1,0:T(8,128)(2,1)S(1)}, u32[]{:S(2)}, u32[]{:S(2)}) %collective-permute-start.5) | collective-permute-done | bytes 98336 | tf_op jit(solution)/shard_map/sum_projections/ppermute | solution.py:360
  72.9 0.0 copy-done.3
  72.9 0.1 sum_projections.3
  73.0 16.6 %all-gather.1 = bf16[512,256]{1,0:T(8,128)(2,1)S(1)} all-gather(bf16[128,256]{1,0:T(8,128)(2,1)S(1)} %sum_projections.3), channel_id=3, replica_groups={{0,128,256,384},{32,160,288,416},{64,192,320,448},{96,224,352,480},{8,1..., dimensions={0}, use_global_device_ids=true | all-gather | bytes 327680 | tf_op jit(solution)/shard_map/gather_keys_values/all_gather | solution.py:352
  89.6 0.0 collective-permute-done.6.refs_2_.refs_4_.refs_6_
  89.6 1.9 %collective-permute-start.7 = (bf16[4,128,256]{2,1,0:T(8,128)(2,1)S(1)}, bf16[4,128,256]{2,1,0:T(8,128)(2,1)S(1)}, u32[]{:S(2)}, u32[]{:S(2)}) collective-permute-start(bf16[4,128,256]{2,1,0:T(8,128)(2,1)S(1)} %bitcast.16), channel_id=1, source_target_pairs={{0,32},{8,40},{16,48},{24,56},{32,64},{40,72},{48,80},{56,88},{64,... | collective-permute-start | bytes 786440 | tf_op jit(solution)/shard_map/gather_keys_values/ppermute | solution.py:343
  91.5 4.6 %collective-permute-start.8 = (bf16[4,128,256]{2,1,0:T(8,128)(2,1)S(1)}, bf16[4,128,256]{2,1,0:T(8,128)(2,1)S(1)}, u32[]{:S(2)}, u32[]{:S(2)}) collective-permute-start(bf16[4,128,256]{2,1,0:T(8,128)(2,1)S(1)} %bitcast.17), channel_id=1, source_target_pairs={{0,480},{8,488},{16,496},{24,504},{32,0},{40,8},{48,16},{56,24},{6... | collective-permute-start | bytes 786440 | tf_op jit(solution)/shard_map/gather_keys_values/ppermute | solution.py:343
  96.1 1.9 %collective-permute-start.9 = (bf16[4,128,256]{2,1,0:T(8,128)(2,1)S(1)}, bf16[4,128,256]{2,1,0:T(8,128)(2,1)S(1)}, u32[]{:S(2)}, u32[]{:S(2)}) collective-permute-start(bf16[4,128,256]{2,1,0:T(8,128)(2,1)S(1)} %bitcast.18), channel_id=1, source_target_pairs={{0,64},{8,456},{16,80},{24,472},{32,96},{40,488},{48,112},{56,504}... | collective-permute-start | bytes 786440 | tf_op jit(solution)/shard_map/gather_keys_values/ppermute | solution.py:343
  98.1 0.0 copy-done.2
  98.1 4.2 %attend.2 = (bf16[512,1024]{1,0:T(8,128)(2,1)S(1)}, f32[512,128]{1,0:T(8,128)S(1)}, bf16[512,128]{1,0:T(8,128)(2,1)S(1)}) custom-call(s32[24]{0:T(128)S(1)} %copy-done.2, s32[128]{0:T(128)S(1)} %copy-done.4, s32[2]{0:T(128)S(1)} %pad_add_fusion.place_ref, bf16[4,128,256]{2,1,0:T(8,128)(2,1)S(1)} %bitcast.19, ...), custom_call_target="tpu_custom_call" | custom-call | flops 2147483648 | bytes 2359296 | tf_op jit(solution)/shard_map/attend/pallas_call | solution.py:486
  102.3 0.0 collective-permute-done.7.refs_0_
  102.3 0.0 collective-permute-done.8.refs_1_
  102.3 6.8 %collective-permute-done.9.refs_2_ = bf16[4,128,256]{2,1,0:T(8,128)(2,1)S(1)} collective-permute-done((bf16[4,128,256]{2,1,0:T(8,128)(2,1)S(1)}, bf16[4,128,256]{2,1,0:T(8,128)(2,1)S(1)}, u32[]{:S(2)}, u32[]{:S(2)}) %collective-permute-start.9) | collective-permute-done | bytes 262176 | tf_op jit(solution)/shard_map/gather_keys_values/ppermute | solution.py:343
  109.2 5.0 %attend.3 = (bf16[256,1152]{1,0:T(8,128)(2,1)S(1)}, bf16[256,1152]{1,0:T(8,128)(2,1)S(1)}) custom-call(s32[24]{0:T(128)S(1)} %copy-done.2, s32[128]{0:T(128)S(1)} %copy-done.4, s32[2]{0:T(128)S(1)} %pad_add_fusion.place_ref, bf16[4,128,256]{2,1,0:T(8,128)(2,1)S(1)} %collective-permute-done.7.refs_0_, ...), custom_call_target="tpu_custom_call" | custom-call | flops 6442450944 | bytes 2359296 | tf_op jit(solution)/shard_map/attend/pallas_call | solution.py:511
  114.1 6.2 %collective-permute-start.10 = (bf16[256,1152]{1,0:T(8,128)(2,1)S(1)}, bf16[256,1152]{1,0:T(8,128)(2,1)S(1)}, u32[]{:S(2)}, u32[]{:S(2)}) collective-permute-start(bf16[256,1152]{1,0:T(8,128)(2,1)S(1)} %get-tuple-element.28), channel_id=1, source_target_pairs={{0,8},{8,0},{16,24},{24,16},{32,40},{40,32},{48,56},{56,48},{64,72... | collective-permute-start | bytes 1769480 | tf_op jit(solution)/shard_map/attend/ppermute | solution.py:360
  120.3 1.6 %collective-permute-done.10.came_ref.core_ref = bf16[256,1152]{1,0:T(8,128)(2,1)S(1)} collective-permute-done((bf16[256,1152]{1,0:T(8,128)(2,1)S(1)}, bf16[256,1152]{1,0:T(8,128)(2,1)S(1)}, u32[]{:S(2)}, u32[]{:S(2)}) %collective-permute-start.10) | collective-permute-done | bytes 589856 | tf_op jit(solution)/shard_map/attend/ppermute | solution.py:360
  121.9 0.2 sum_attention.2
  122.2 3.0 %collective-permute-start.11 = (bf16[128,1152]{1,0:T(8,128)(2,1)S(1)}, bf16[128,1152]{1,0:T(8,128)(2,1)S(1)}, u32[]{:S(2)}, u32[]{:S(2)}) collective-permute-start(bf16[128,1152]{1,0:T(8,128)(2,1)S(1)} %sum_attention.2), channel_id=1, source_target_pairs={{0,16},{8,24},{16,0},{24,8},{32,48},{40,56},{48,32},{56,40},{64,80... | collective-permute-start | bytes 884744 | tf_op jit(solution)/shard_map/sum_attention/ppermute | solution.py:360
  125.8 8.0 %collective-permute-done.11.chip_ref = bf16[128,1152]{1,0:T(8,128)(2,1)S(1)} collective-permute-done((bf16[128,1152]{1,0:T(8,128)(2,1)S(1)}, bf16[128,1152]{1,0:T(8,128)(2,1)S(1)}, u32[]{:S(2)}, u32[]{:S(2)}) %collective-permute-start.11) | collective-permute-done | bytes 294944 | tf_op jit(solution)/shard_map/sum_attention/ppermute | solution.py:360
  133.8 1.6 %sum_attention.3 = bf16[128,1024]{1,0:T(8,128)(2,1)} custom-call(s32[24]{0:T(128)S(1)} %copy-done.2, s32[2]{0:T(128)S(1)} %pad_add_fusion.place_ref, f32[1,1]{1,0:T(1,128)} %bitcast.9.gate_ref, bf16[256,1152]{1,0:T(8,128)(2,1)S(1)} %get-tuple-element.27.kept_ref, bf16[256,1152]{1,0:T(8,128)(2,1)S(1)} %collective-permute-done.10.came_ref.core_ref, ...), custom_call_target="tpu_custom_call" | custom-call | tf_op jit(solution)/shard_map/sum_attention/pallas_call | solution.py:551
  (7 shorter events, 0.1 us)
Async XLA Ops:
  2.6 10.8 %copy-start = (bf16[128,1024]{1,0:T(8,128)(2,1)S(1)}, bf16[128,1024]{1,0:T(8,128)(2,1)}, u32[]{:S(2)}) copy-start(bf16[128,1024]{1,0:T(8,128)(2,1)} %q_ref.1) | copy-start | bytes 786436
  2.6 10.8 %copy-start.1 = (f32[128]{0:T(128)S(1)}, f32[128]{0:T(128)}, u32[]{:S(2)}) copy-start(f32[128]{0:T(128)} %param.10) | copy-start | bytes 1540
  2.6 13.2 %copy-start.5 = (bf16[128,128]{1,0:T(8,128)(2,1)S(1)}, bf16[128,128]{1,0:T(8,128)(2,1)}, u32[]{:S(2)}) copy-start(bf16[128,128]{1,0:T(8,128)(2,1)} %param.15) | copy-start | bytes 98308
  2.6 13.2 %copy-start.6 = (bf16[128,128]{1,0:T(8,128)(2,1)S(1)}, bf16[128,128]{1,0:T(8,128)(2,1)}, u32[]{:S(2)}) copy-start(bf16[128,128]{1,0:T(8,128)(2,1)} %param.14) | copy-start | bytes 98308
  2.6 44.5 %all-to-all-start = ((bf16[32,2,128,128]{3,2,1,0:T(8,128)(2,1)}), bf16[32,2,128,128]{3,2,1,0:T(8,128)(2,1)S(1)}, u32[]{:S(2)}, u32[]{:S(2)}) async-start(bf16[32,2,128,128]{3,2,1,0:T(8,128)(2,1)} %bitcast.22), calls=%async_computation | async-start | bytes 4194304 | tf_op jit(solution)/shard_map/spread_vision/all_to_all | solution.py:416
  13.6 33.5 %collective-permute-start = (bf16[8,128,128]{2,1,0:T(8,128)(2,1)S(1)}, bf16[8,128,128]{2,1,0:T(8,128)(2,1)}, u32[]{:S(2)}, u32[]{:S(2)}) collective-permute-start(bf16[8,128,128]{2,1,0:T(8,128)(2,1)S(1)} %norm_queries.1.refs_1_.refs_3_), channel_id=1, source_target_pairs={{0,8},{8,0},{16,24},{24,16},{32,40},{40,32},{48,56},{56,48},{64,72... | collective-permute-start | bytes 786440 | tf_op jit(solution)/shard_map/share_queries/ppermute | solution.py:360
  38.7 15.0 %collective-permute-start.2 = (bf16[4,128,256]{2,1,0:T(8,128)(2,1)S(1)}, bf16[4,128,256]{2,1,0:T(8,128)(2,1)S(1)}, u32[]{:S(2)}, u32[]{:S(2)}) collective-permute-start(bf16[4,128,256]{2,1,0:T(8,128)(2,1)S(1)} %bitcast.12), channel_id=1, source_target_pairs={{0,32},{8,40},{16,48},{24,56},{32,64},{40,72},{48,80},{56,88},{64,... | collective-permute-start | bytes 786440 | tf_op jit(solution)/shard_map/gather_projections/ppermute | solution.py:343
  41.3 12.3 %collective-permute-start.3 = (bf16[4,128,256]{2,1,0:T(8,128)(2,1)S(1)}, bf16[4,128,256]{2,1,0:T(8,128)(2,1)S(1)}, u32[]{:S(2)}, u32[]{:S(2)}) collective-permute-start(bf16[4,128,256]{2,1,0:T(8,128)(2,1)S(1)} %bitcast.13), channel_id=1, source_target_pairs={{0,480},{8,488},{16,496},{24,504},{32,0},{40,8},{48,16},{56,24},{6... | collective-permute-start | bytes 786440 | tf_op jit(solution)/shard_map/gather_projections/ppermute | solution.py:343
  45.2 13.2 %collective-permute-start.1 = (bf16[4,128,256]{2,1,0:T(8,128)(2,1)S(1)}, bf16[4,128,256]{2,1,0:T(8,128)(2,1)S(1)}, u32[]{:S(2)}, u32[]{:S(2)}) collective-permute-start(bf16[4,128,256]{2,1,0:T(8,128)(2,1)S(1)} %bitcast.14), channel_id=1, source_target_pairs={{0,64},{8,456},{16,80},{24,472},{32,96},{40,488},{48,112},{56,504}... | collective-permute-start | bytes 786440 | tf_op jit(solution)/shard_map/gather_projections/ppermute | solution.py:343
  48.9 40.7 %collective-permute-start.6 = (bf16[16,128,128]{2,1,0:T(8,128)(2,1)}, bf16[16,128,128]{2,1,0:T(8,128)(2,1)}, u32[]{:S(2)}, u32[]{:S(2)}) collective-permute-start(bf16[16,128,128]{2,1,0:T(8,128)(2,1)} %pad_maximum_fusion), channel_id=1, source_target_pairs={{0,16},{8,24},{16,0},{24,8},{32,48},{40,56},{48,32},{56,40},{64,80... | collective-permute-start | bytes 1572872 | tf_op jit(solution)/shard_map/share_queries/ppermute | solution.py:360
  54.8 18.1 %copy-start.3 = (f32[128]{0:T(128)S(1)}, f32[128]{0:T(128)}, u32[]{:S(2)}) copy-start(f32[128]{0:T(128)} %param.11) | copy-start | bytes 1540
  54.8 43.2 %copy-start.2 = (s32[24]{0:T(128)S(1)}, s32[24]{0:T(128)}, u32[]{:S(2)}) copy-start(s32[24]{0:T(128)} %image_start_ref.5) | copy-start | bytes 292
  54.8 43.2 %copy-start.4 = (s32[128]{0:T(128)S(1)}, s32[128]{0:T(128)}, u32[]{:S(2)}) copy-start(s32[128]{0:T(128)} %slot_image_ref.3) | copy-start | bytes 1540
  59.2 5.9 %collective-permute-start.4 = (bf16[256,384]{1,0:T(8,128)(2,1)S(1)}, bf16[256,384]{1,0:T(8,128)(2,1)S(1)}, u32[]{:S(2)}, u32[]{:S(2)}) collective-permute-start(bf16[256,384]{1,0:T(8,128)(2,1)S(1)} %get-tuple-element.19), channel_id=1, source_target_pairs={{0,8},{8,0},{16,24},{24,16},{32,40},{40,32},{48,56},{56,48},{64,72... | collective-permute-start | bytes 589832 | tf_op jit(solution)/shard_map/sum_projections/ppermute | solution.py:360
  65.2 7.7 %collective-permute-start.5 = (bf16[128,384]{1,0:T(8,128)(2,1)S(1)}, bf16[128,384]{1,0:T(8,128)(2,1)S(1)}, u32[]{:S(2)}, u32[]{:S(2)}) collective-permute-start(bf16[128,384]{1,0:T(8,128)(2,1)S(1)} %sum_projections.2), channel_id=1, source_target_pairs={{0,16},{8,24},{16,0},{24,8},{32,48},{40,56},{48,32},{56,40},{64,80... | collective-permute-start | bytes 294920 | tf_op jit(solution)/shard_map/sum_projections/ppermute | solution.py:360
  89.6 12.7 %collective-permute-start.7 = (bf16[4,128,256]{2,1,0:T(8,128)(2,1)S(1)}, bf16[4,128,256]{2,1,0:T(8,128)(2,1)S(1)}, u32[]{:S(2)}, u32[]{:S(2)}) collective-permute-start(bf16[4,128,256]{2,1,0:T(8,128)(2,1)S(1)} %bitcast.16), channel_id=1, source_target_pairs={{0,32},{8,40},{16,48},{24,56},{32,64},{40,72},{48,80},{56,88},{64,... | collective-permute-start | bytes 786440 | tf_op jit(solution)/shard_map/gather_keys_values/ppermute | solution.py:343
  91.5 10.8 %collective-permute-start.8 = (bf16[4,128,256]{2,1,0:T(8,128)(2,1)S(1)}, bf16[4,128,256]{2,1,0:T(8,128)(2,1)S(1)}, u32[]{:S(2)}, u32[]{:S(2)}) collective-permute-start(bf16[4,128,256]{2,1,0:T(8,128)(2,1)S(1)} %bitcast.17), channel_id=1, source_target_pairs={{0,480},{8,488},{16,496},{24,504},{32,0},{40,8},{48,16},{56,24},{6... | collective-permute-start | bytes 786440 | tf_op jit(solution)/shard_map/gather_keys_values/ppermute | solution.py:343
  96.1 13.0 %collective-permute-start.9 = (bf16[4,128,256]{2,1,0:T(8,128)(2,1)S(1)}, bf16[4,128,256]{2,1,0:T(8,128)(2,1)S(1)}, u32[]{:S(2)}, u32[]{:S(2)}) collective-permute-start(bf16[4,128,256]{2,1,0:T(8,128)(2,1)S(1)} %bitcast.18), channel_id=1, source_target_pairs={{0,64},{8,456},{16,80},{24,472},{32,96},{40,488},{48,112},{56,504}... | collective-permute-start | bytes 786440 | tf_op jit(solution)/shard_map/gather_keys_values/ppermute | solution.py:343
  114.1 7.8 %collective-permute-start.10 = (bf16[256,1152]{1,0:T(8,128)(2,1)S(1)}, bf16[256,1152]{1,0:T(8,128)(2,1)S(1)}, u32[]{:S(2)}, u32[]{:S(2)}) collective-permute-start(bf16[256,1152]{1,0:T(8,128)(2,1)S(1)} %get-tuple-element.28), channel_id=1, source_target_pairs={{0,8},{8,0},{16,24},{24,16},{32,40},{40,32},{48,56},{56,48},{64,72... | collective-permute-start | bytes 1769480 | tf_op jit(solution)/shard_map/attend/ppermute | solution.py:360
  122.2 11.6 %collective-permute-start.11 = (bf16[128,1152]{1,0:T(8,128)(2,1)S(1)}, bf16[128,1152]{1,0:T(8,128)(2,1)S(1)}, u32[]{:S(2)}, u32[]{:S(2)}) collective-permute-start(bf16[128,1152]{1,0:T(8,128)(2,1)S(1)} %sum_attention.2), channel_id=1, source_target_pairs={{0,16},{8,24},{16,0},{24,8},{32,48},{40,56},{48,32},{56,40},{64,80... | collective-permute-start | bytes 884744 | tf_op jit(solution)/shard_map/sum_attention/ppermute | solution.py:360
where the time goes:
time: 136 us; the launch traced here: 135 us
  starting transfers between devices  53.5 us (39%)
  blocking collectives  39.4 us (29%)
  waiting for transfers between devices  23.7 us (17%)
  Pallas kernels  15.9 us (12%)
  other arithmetic  1.88 us (1%)
    all_gather x2, blocking collectives, gather_along_z(): own = lax.all_gather(block, 'ctx', axis_index_groups=groups)  39.4 us
    ppermute x6, starting transfers between devices, other_member(): return lax.ppermute(value, 'ctx', [(i, i ^ mask) for i in range(ctx_size)])  26 us
    ppermute x6, starting transfers between devices, shift(): lax.ppermute(value, 'ctx', [(i, (i + moves[i]) % ctx_size) for i in range...  16.8 us
    ppermute x6, waiting for transfers between devices, other_member(): return lax.ppermute(value, 'ctx', [(i, i ^ mask) for i in range(ctx_size)])  13.3 us
    all_to_all x1, starting transfers between devices, local(): lax.all_to_all(mine, ('ctx', 'head'), 0, 0, axis_index_groups=whole_plane)  10.7 us
    ppermute x6, waiting for transfers between devices, shift(): lax.ppermute(value, 'ctx', [(i, (i + moves[i]) % ctx_size) for i in range...  10.4 us
    pallas_call x1, Pallas kernels, local(): pl.pallas_call(functools.partial(attend_last_kernel, scale=scale, group=g...  4.96 us
    pallas_call x1, Pallas kernels, local(): pl.pallas_call(functools.partial(attend_first_kernel, scale=scale, slots_...  4.22 us
  transfers between devices with their start and end apart: 13, of which 6 were waited for; matrix products, arithmetic and copies ran while one was open for 1% of the time, Pallas kernels for 5%

commit v1 on v0

--- a/solution.py
+++ b/solution.py
@@ -12,11 +12,12 @@
 PLANE = 4
 VMEM_LIMIT = 16 * 1024 * 1024
 SPREAD_LIMIT = 62 * 1024 * 1024
+NO_IMAGE = 127
 HIDE = -30000.0
 STRIDE = 4
-SOURCES = ((0, (0, 1, 2, 3)), (-1, (0, 1, 2, 3)), (1, (0, 1, 2, 3)), (2, (0, 1, 2, 3)))
-
-FIRST = 3
+SOURCES = ((0, (0, 1, 2, 3)), (2, (0, 1, 2, 3)), (-1, (0, 1, 2, 3)), (1, (0, 1, 2, 3)))
+
+FIRST = 2
 
 
 def source_rank(plane_rank, step, turn):
@@ -41,14 +42,13 @@
     for member in range(members):
         for block in range(blocks):
             first = (block * members + member) * width
-            pieces_ref[member, block] = x_ref[:, first : first + width]
-        for peer in range(peers):
-            copies.append(
-                pltpu.make_async_copy(
-                    pieces_ref.at[member], out_ref.at[member, peer], sems.at[len(copies)]
-                )
-            )
-            copies[-1].start()
+            piece = x_ref[:, first : first + width]
+            for peer in range(peers):
+                pieces_ref[member, peer, block] = piece
+        copies.append(
+            pltpu.make_async_copy(pieces_ref.at[member], out_ref.at[member], sems.at[member])
+        )
+        copies[-1].start()
     for copy in copies:
         copy.wait()
 
@@ -157,43 +157,42 @@
     values_ref[to] = jnp.concatenate([kv_ref[at, rows, head_dim:], ones], axis=1)
 
 
-def weigh(q_refs, halves, heads, several, late, keys, values, scale):
-    q = [
-        jnp.concatenate(
-            [
-                jnp.concatenate(
-                    [ref[half * heads + head] for ref, half in zip(q_refs, halves)], axis=0
-                ),
-                late,
-            ],
-            axis=1,
-        )
-        for head in several
-    ]
+def weigh(queries, keys, values, scale):
     scores = lax.dot_general(
-        jnp.concatenate(q, axis=0),
-        keys,
-        (((1,), (1,)), ((), ())),
-        preferred_element_type=jnp.float32,
+        queries, keys, (((1,), (1,)), ((), ())), preferred_element_type=jnp.float32
     )
     weights = jnp.exp2(scores * scale).astype(jnp.bfloat16)
-    total = jnp.dot(weights, values, preferred_element_type=jnp.float32)
-    rows = late.shape[0]
-    return [total[i * rows : (i + 1) * rows] for i in range(len(several))]
+    return jnp.dot(weights, values, preferred_element_type=jnp.float32)
 
 
 def attend_first_kernel(
-    image_start_ref, slot_image_ref, place_ref, *refs, scale, slots_here, heads, halves
+    image_start_ref, slot_image_ref, place_ref, *refs, scale, slots_here, halves
 ):
     kv_ref, q_refs = refs[0], refs[1 : 1 + PLANE]
-    numer_ref, sums_ref, late_ref, keys_ref, values_ref = refs[1 + PLANE :]
+    numer_ref, sums_ref, marked_ref, plan_ref, keys_ref, values_ref = refs[1 + PLANE :]
     _, own, head_dim = q_refs[0].shape
+    heads = marked_ref.shape[0]
     n_images = image_start_ref.shape[0]
     tokens = PLANE * own
     plane_rank = place_ref[0]
     member = place_ref[1]
     first_token = plane_rank * tokens
     total_tokens = tokens * (slot_image_ref.shape[0] // (slots_here * PLANE))
+
+    kept = jnp.int32(0)
+    number = 0
+    for step, several in SOURCES[1:]:
+        for turn in several:
+            rank = source_rank(plane_rank, step, turn)
+            for here in range(slots_here):
+                image = slot_image_ref[(rank * PLANE + member) * slots_here + here]
+                start = image_start_ref[jnp.minimum(image, n_images - 1)]
+                seen = jnp.logical_and(image < n_images, start < first_token + tokens)
+                plan_ref[2 * number] = image
+                plan_ref[2 * number + 1] = jnp.where(seen, kept, -1)
+                kept = kept + seen.astype(jnp.int32)
+                number += 1
+    plan_ref[2 * number] = kept
 
     lane = lax.broadcasted_iota(jnp.int32, (own, head_dim), 1)
     starts = jnp.full((own, head_dim), total_tokens, jnp.int32)
@@ -203,9 +202,11 @@
         position = (
             first_token + one * own + lax.broadcasted_iota(jnp.int32, (own, head_dim), 0)
         )
-        late_ref[at * own : (at + 1) * own] = jnp.where(starts > position, 1.0, 0.0).astype(
-            jnp.bfloat16
-        )
+        late = jnp.where(starts > position, 1.0, 0.0).astype(jnp.bfloat16)
+        rows = slice(at * own, (at + 1) * own)
+        for head in range(heads):
+            marked_ref[head, rows, :head_dim] = q_refs[at][halves[at] * heads + head]
+            marked_ref[head, rows, head_dim:] = late
 
     step, several = SOURCES[0]
     for at, turn in enumerate(several):
@@ -217,60 +218,49 @@
     column = lax.broadcasted_iota(jnp.int32, sums_ref.shape, 1)
     keys = keys_ref[...].reshape(-1, 2 * head_dim)
     values = values_ref[...].reshape(-1, 2 * head_dim)
-    together = 2
-
-    def some_heads(number, _):
-        several = [number * together + i for i in range(together)]
-        totals = weigh(q_refs, halves, heads, several, late_ref[...], keys, values, scale)
-        sums = sums_ref[...]
-        for head, total in zip(several, totals):
-            at = pl.ds(pl.multiple_of(head * head_dim, head_dim), head_dim)
-            numer_ref[:, at] = total[:, :head_dim].astype(numer_ref.dtype)
-            sums = jnp.where(column == head, total[:, head_dim:], sums)
-        sums_ref[...] = sums
+
+    def one_head(head, _):
+        total = weigh(marked_ref[head], keys, values, scale)
+        at = pl.ds(pl.multiple_of(head * head_dim, head_dim), head_dim)
+        numer_ref[:, at] = total[:, :head_dim].astype(numer_ref.dtype)
+        sums_ref[...] = jnp.where(column == head, total[:, head_dim:], sums_ref[...])
         return 0
 
-    lax.fori_loop(0, heads // together, some_heads, 0, unroll=2)
-
-
-def attend_last_kernel(
-    image_start_ref, slot_image_ref, place_ref, *refs, scale, group, slots_here, heads, halves
-):
+    lax.fori_loop(0, heads, one_head, 0, unroll=2)
+
+
+def attend_last_kernel(plan_ref, *refs, scale, group, slots_here):
     sources = SOURCES[1:]
-    kv_refs, q_refs = refs[: len(sources)], refs[len(sources) : len(sources) + PLANE]
-    numer_ref, came_ref, late_ref, kept_ref, to_core_ref = refs[len(sources) + PLANE : -3]
+    kv_refs = refs[: len(sources)]
+    numer_ref, came_ref, marked_ref, kept_ref, to_core_ref = refs[len(sources) : -3]
     keys_ref, values_ref, sums_ref = refs[-3:]
-    _, own, head_dim = q_refs[0].shape
-    n_images = image_start_ref.shape[0]
-    plane_rank = place_ref[0]
-    limit = (plane_rank + 1) * PLANE * own
+    heads, tokens, width = marked_ref.shape
+    head_dim = width // 2
 
     put = functools.partial(put_slot, keys_ref, values_ref)
-    kept = jnp.int32(0)
-    for kv_ref, (step, several) in zip(kv_refs, sources):
-        for at, turn in enumerate(several):
-            rank = source_rank(plane_rank, step, turn)
+    number = 0
+    for kv_ref, (_, several) in zip(kv_refs, sources):
+        for at in range(len(several)):
             for here in range(slots_here):
-                image = slot_image_ref[(rank * PLANE + place_ref[1]) * slots_here + here]
-                start = image_start_ref[jnp.minimum(image, n_images - 1)]
-                seen = jnp.logical_and(image < n_images, start < limit)
-                pl.when(seen)(functools.partial(put, kept, kv_ref, at, here, image))
-                kept = kept + seen.astype(jnp.int32)
+                image, to = plan_ref[2 * number], plan_ref[2 * number + 1]
+                pl.when(to >= 0)(functools.partial(put, to, kv_ref, at, here, image))
+                number += 1
+    kept = plan_ref[2 * number]
     turns = (kept + group - 1) // group
 
     def fill(to, _):
-        put(to, kv_refs[0], 0, 0, n_images)
+        put(to, kv_refs[0], 0, 0, NO_IMAGE)
         return 0
 
     lax.fori_loop(kept, turns * group, fill, 0)
     sums_ref[...] = came_ref[...]
     column = lax.broadcasted_iota(jnp.int32, sums_ref.shape, 1)
-    half = 2 * own
+    half = tokens // 2
 
     def one_head(head, _, count):
         keys = keys_ref[:count].reshape(-1, 2 * head_dim)
         values = values_ref[:count].reshape(-1, 2 * head_dim)
-        [total] = weigh(q_refs, halves, heads, [head], late_ref[...], keys, values, scale)
+        total = weigh(marked_ref[head], keys, values, scale)
         at = pl.ds(pl.multiple_of(head * head_dim, head_dim), head_dim)
         numer = (numer_ref[:, at].astype(jnp.float32) + total[:, :head_dim]).astype(jnp.bfloat16)
         kept_ref[:, at] = numer[:half]
@@ -352,7 +342,7 @@
     own = lax.all_gather(block, "ctx", axis_index_groups=groups)
     if beside is not None:
         own, beside = lax.optimization_barrier((own, beside))
-    return (own, shift(own, 1), shift(own, -1), shift(own, 2, -2)), beside
+    return (own, shift(own, 2, -2), shift(own, 1), shift(own, -1)), beside
 
 
 def other_member(value, mask):
@@ -407,8 +397,8 @@
             in_specs=[vmem()],
             out_specs=pl.BlockSpec(memory_space=pltpu.HBM),
             scratch_shapes=[
-                pltpu.VMEM((PLANE, blocks, rows, piece_rows), jnp.bfloat16),
-                pltpu.SemaphoreType.DMA((PLANE * head_size,)),
+                pltpu.VMEM((PLANE, head_size, blocks, rows, piece_rows), jnp.bfloat16),
+                pltpu.SemaphoreType.DMA((PLANE,)),
             ],
             compiler_params=pltpu.CompilerParams(vmem_limit_bytes=SPREAD_LIMIT),
         )(vision)
@@ -483,21 +473,21 @@
                 transcendentals=scores,
             )
 
-        numer, sums, late = pl.pallas_call(
+        numer, sums, marked, plan = pl.pallas_call(
             functools.partial(
                 attend_first_kernel,
                 scale=scale,
                 slots_here=slots_here,
-                heads=heads,
                 halves=tuple(half for _, half in plane_queries),
             ),
             out_shape=[
                 jax.ShapeDtypeStruct((PLANE * tokens, q_cols), jnp.bfloat16),
                 jax.ShapeDtypeStruct((PLANE * tokens, head_dim), jnp.float32),
-                jax.ShapeDtypeStruct((PLANE * tokens, head_dim), jnp.bfloat16),
+                jax.ShapeDtypeStruct((heads, PLANE * tokens, 2 * head_dim), jnp.bfloat16),
+                jax.ShapeDtypeStruct((2 * last_slots + 1,), jnp.int32),
             ],
             in_specs=[smem()] * 3 + [vmem()] * (1 + PLANE),
-            out_specs=[vmem()] * 3,
+            out_specs=[vmem()] * 3 + [smem()],
             scratch_shapes=[pltpu.VMEM((slots, tile_rows, 2 * head_dim), jnp.bfloat16)] * 2,
             compiler_params=params(),
             cost_estimate=cost(PLANE * tokens, slots),
@@ -510,15 +500,10 @@
         )
         own_and_chip, to_core = pl.pallas_call(
             functools.partial(
-                attend_last_kernel,
-                scale=scale,
-                group=group,
-                slots_here=slots_here,
-                heads=heads,
-                halves=tuple(half for _, half in plane_queries),
+                attend_last_kernel, scale=scale, group=group, slots_here=slots_here
             ),
             out_shape=[jax.ShapeDtypeStruct((2 * tokens, width), jnp.bfloat16)] * 2,
-            in_specs=[smem()] * 3 + [vmem()] * (len(all_kv) - 1 + PLANE + 3),
+            in_specs=[smem()] + [vmem()] * (len(all_kv) - 1 + 3),
             out_specs=[vmem()] * 2,
             scratch_shapes=[
                 pltpu.VMEM((last_slots, tile_rows, 2 * head_dim), jnp.bfloat16),
@@ -527,16 +512,7 @@
             ],
             compiler_params=params(),
             cost_estimate=cost(PLANE * tokens, last_slots),
-        )(
-            image_start,
-            slot_image,
-            place,
-            *all_kv[1:],
-            *(source for source, _ in plane_queries),
-            numer,
-            sums,
-            late,
-        )
+        )(plan, *all_kv[1:], numer, sums, marked)
         from_core = other_member(to_core, 1)
 
     with jax.named_scope("sum_attention"):

time: 136 us -> 130 us (0.956)
  waiting for transfers between devices: 23.7 us -> 15.1 us
  starting transfers between devices: 53.5 us -> 59.1 us
  Pallas kernels: 15.9 us -> 13.3 us
    ppermute x6, waiting for transfers between devices: 10.4 us -> 1.5 us  [shift(): lax.ppermute(value, 'ctx', [(i, (i + moves[i]) % ctx_size) for i in range...]
    pallas_call x1, Pallas kernels: 4.96 us -> 0.98 us  [local(): pl.pallas_call(functools.partial(attend_last_kernel, scale=scale, group=g...]
    ppermute x6, starting transfers between devices: 26 us -> 29.4 us  [other_member(): return lax.ppermute(value, 'ctx', [(i, i ^ mask) for i in range(ctx_size)])]
    ppermute x6, starting transfers between devices: 16.8 us -> 19 us  [shift(): lax.ppermute(value, 'ctx', [(i, (i + moves[i]) % ctx_size) for i in range...]
  transfers between devices with their start and end apart: 13 -> 13, of which waited for: 6 -> 5; matrix products, arithmetic and copies ran while one was open for 1% -> 1% of each run, Pallas kernels for 5% -> 6%
where the time goes in v1:
time: 130 us; the launch traced here: 129 us
  starting transfers between devices  59.1 us (45%)
  blocking collectives  39.5 us (30%)
  waiting for transfers between devices  15.1 us (12%)
  Pallas kernels  13.3 us (10%)
    all_gather x2, blocking collectives, gather_along_z(): own = lax.all_gather(block, 'ctx', axis_index_groups=groups)  39.5 us
    ppermute x6, starting transfers between devices, other_member(): return lax.ppermute(value, 'ctx', [(i, i ^ mask) for i in range(ctx_size)])  29.4 us
    ppermute x6, starting transfers between devices, shift(): lax.ppermute(value, 'ctx', [(i, (i + moves[i]) % ctx_size) for i in range...  19 us
    ppermute x6, waiting for transfers between devices, other_member(): return lax.ppermute(value, 'ctx', [(i, i ^ mask) for i in range(ctx_size)])  13.6 us
    all_to_all x1, starting transfers between devices, local(): lax.all_to_all(mine, ('ctx', 'head'), 0, 0, axis_index_groups=whole_plane)  10.7 us
    pallas_call x1, Pallas kernels, local(): pl.pallas_call(functools.partial(attend_first_kernel, scale=scale, slots_...  5.44 us
  transfers between devices with their start and end apart: 13, of which 5 were waited for; matrix products, arithmetic and copies ran while one was open for 1% of the time, Pallas kernels for 6%

profile of v1, /device:TPU:1, one launch (start us, length us, event | category | flops | bytes accessed | tf_op | source)
XLA Modules:
  0.0 128.9 jit_solution(9219614333087829052)
XLA Ops:
  0.0 2.4 %spread_vision.1 = bf16[4,8,2,128,128]{4,3,2,1,0:T(8,128)(2,1)} custom-call(bf16[128,1024]{1,0:T(8,128)(2,1)} %x_ref.1), custom_call_target="tpu_custom_call" | custom-call | tf_op jit(solution)/shard_map/spread_vision/pallas_call | solution.py:392
  2.4 0.0 copy-start
  2.4 0.0 copy-start.1
  2.4 0.0 copy-start.5
  2.4 0.0 copy-start.6
  2.4 10.7 %all-to-all-start = ((bf16[32,2,128,128]{3,2,1,0:T(8,128)(2,1)}), bf16[32,2,128,128]{3,2,1,0:T(8,128)(2,1)S(1)}, u32[]{:S(2)}, u32[]{:S(2)}) async-start(bf16[32,2,128,128]{3,2,1,0:T(8,128)(2,1)} %bitcast.22), calls=%async_computation | async-start | bytes 4194304 | tf_op jit(solution)/shard_map/spread_vision/all_to_all | solution.py:406
  13.2 0.0 copy-done
  13.2 0.0 copy-done.1
  13.2 0.2 norm_queries.1.refs_1_
  13.4 2.2 %collective-permute-start = (bf16[8,128,128]{2,1,0:T(8,128)(2,1)S(1)}, bf16[8,128,128]{2,1,0:T(8,128)(2,1)S(1)}, u32[]{:S(2)}, u32[]{:S(2)}) collective-permute-start(bf16[8,128,128]{2,1,0:T(8,128)(2,1)S(1)} %norm_queries.1.refs_1_), channel_id=1, source_target_pairs={{0,8},{8,0},{16,24},{24,16},{32,40},{40,32},{48,56},{56,48},{64,72... | collective-permute-start | bytes 786440 | tf_op jit(solution)/shard_map/share_queries/ppermute | solution.py:350
  15.7 22.8 %all-gather = bf16[512,256]{1,0:T(8,128)(2,1)S(1)} all-gather(bf16[128,256]{1,0:T(8,128)(2,1)S(1)} %pad_maximum_fusion.1), channel_id=2, replica_groups={{0,128,256,384},{32,160,288,416},{64,192,320,448},{96,224,352,480},{8,1..., dimensions={0}, use_global_device_ids=true | all-gather | bytes 327680 | tf_op jit(solution)/shard_map/gather_projections/all_gather | solution.py:342
  38.5 3.1 %collective-permute-start.3 = (bf16[4,128,256]{2,1,0:T(8,128)(2,1)S(1)}, bf16[4,128,256]{2,1,0:T(8,128)(2,1)}, u32[]{:S(2)}, u32[]{:S(2)}) collective-permute-start(bf16[4,128,256]{2,1,0:T(8,128)(2,1)S(1)} %bitcast.12), channel_id=1, source_target_pairs={{0,64},{8,456},{16,80},{24,472},{32,96},{40,488},{48,112},{56,504}... | collective-permute-start | bytes 786440 | tf_op jit(solution)/shard_map/gather_projections/ppermute | solution.py:333
  41.6 3.0 %collective-permute-start.1 = (bf16[4,128,256]{2,1,0:T(8,128)(2,1)S(1)}, bf16[4,128,256]{2,1,0:T(8,128)(2,1)S(1)}, u32[]{:S(2)}, u32[]{:S(2)}) collective-permute-start(bf16[4,128,256]{2,1,0:T(8,128)(2,1)S(1)} %bitcast.13), channel_id=1, source_target_pairs={{0,32},{8,40},{16,48},{24,56},{32,64},{40,72},{48,80},{56,88},{64,... | collective-permute-start | bytes 786440 | tf_op jit(solution)/shard_map/gather_projections/ppermute | solution.py:333
  44.6 3.5 %collective-permute-start.2 = (bf16[4,128,256]{2,1,0:T(8,128)(2,1)S(1)}, bf16[4,128,256]{2,1,0:T(8,128)(2,1)S(1)}, u32[]{:S(2)}, u32[]{:S(2)}) collective-permute-start(bf16[4,128,256]{2,1,0:T(8,128)(2,1)S(1)} %bitcast.14), channel_id=1, source_target_pairs={{0,480},{8,488},{16,496},{24,504},{32,0},{40,8},{48,16},{56,24},{6... | collective-permute-start | bytes 786440 | tf_op jit(solution)/shard_map/gather_projections/ppermute | solution.py:333
  48.1 0.0 collective-permute-done.refs_3_
  48.1 0.0 all-to-all-done
  48.1 0.8 pad_maximum_fusion
  48.9 4.7 %collective-permute-start.6 = (bf16[16,128,128]{2,1,0:T(8,128)(2,1)}, bf16[16,128,128]{2,1,0:T(8,128)(2,1)}, u32[]{:S(2)}, u32[]{:S(2)}) collective-permute-start(bf16[16,128,128]{2,1,0:T(8,128)(2,1)} %pad_maximum_fusion), channel_id=1, source_target_pairs={{0,16},{8,24},{16,0},{24,8},{32,48},{40,56},{48,32},{56,40},{64,80... | collective-permute-start | bytes 1572872 | tf_op jit(solution)/shard_map/share_queries/ppermute | solution.py:350
  53.7 0.1 pad_add_fusion.place_ref
  53.7 0.0 collective-permute-done.3.refs_1_
  53.7 1.4 %project.2.refs_2_ = f32[512,256]{1,0:T(8,128)S(1)} custom-call(s32[2]{0:T(128)S(1)} %pad_add_fusion.place_ref, bf16[4,16,128,128]{3,2,1,0:T(8,128)(2,1)S(1)} %bitcast.10, bf16[4,128,256]{2,1,0:T(8,128)(2,1)S(1)} %bitcast.15, bf16[4,128,256]{2,1,0:T(8,128)(2,1)} %collective-permute-done.3.refs_1_), custom_call_target="tpu_custom_call" | custom-call | tf_op jit(solution)/shard_map/project/pallas_call | solution.py:420
  55.1 0.0 copy-start.3
  55.1 0.0 copy-start.2
  55.2 0.0 copy-start.4
  55.2 0.0 collective-permute-done.1.refs_0_
  55.2 0.0 collective-permute-done.2.refs_1_
  55.2 1.0 project.3
  56.2 6.3 %collective-permute-start.4 = (bf16[256,384]{1,0:T(8,128)(2,1)S(1)}, bf16[256,384]{1,0:T(8,128)(2,1)S(1)}, u32[]{:S(2)}, u32[]{:S(2)}) collective-permute-start(bf16[256,384]{1,0:T(8,128)(2,1)S(1)} %get-tuple-element.20), channel_id=1, source_target_pairs={{0,8},{8,0},{16,24},{24,16},{32,40},{40,32},{48,56},{56,48},{64,72... | collective-permute-start | bytes 589832 | tf_op jit(solution)/shard_map/sum_projections/ppermute | solution.py:350
  62.5 1.0 collective-permute-done.4.came_ref.core_ref
  63.6 4.1 %collective-permute-start.5 = (bf16[128,384]{1,0:T(8,128)(2,1)S(1)}, bf16[128,384]{1,0:T(8,128)(2,1)S(1)}, u32[]{:S(2)}, u32[]{:S(2)}) collective-permute-start(bf16[128,384]{1,0:T(8,128)(2,1)S(1)} %sum_projections.2), channel_id=1, source_target_pairs={{0,16},{8,24},{16,0},{24,8},{32,48},{40,56},{48,32},{56,40},{64,80... | collective-permute-start | bytes 294920 | tf_op jit(solution)/shard_map/sum_projections/ppermute | solution.py:350
  67.7 3.3 %collective-permute-done.5.chip_ref = bf16[128,384]{1,0:T(8,128)(2,1)S(1)} collective-permute-done((bf16[128,384]{1,0:T(8,128)(2,1)S(1)}, bf16[128,384]{1,0:T(8,128)(2,1)S(1)}, u32[]{:S(2)}, u32[]{:S(2)}) %collective-permute-start.5) | collective-permute-done | bytes 98336 | tf_op jit(solution)/shard_map/sum_projections/ppermute | solution.py:350
  71.0 0.1 sum_projections.3
  71.1 16.7 %all-gather.1 = bf16[512,256]{1,0:T(8,128)(2,1)S(1)} all-gather(bf16[128,256]{1,0:T(8,128)(2,1)S(1)} %sum_projections.3), channel_id=3, replica_groups={{0,128,256,384},{32,160,288,416},{64,192,320,448},{96,224,352,480},{8,1..., dimensions={0}, use_global_device_ids=true | all-gather | bytes 327680 | tf_op jit(solution)/shard_map/gather_keys_values/all_gather | solution.py:342
  87.8 0.0 collective-permute-done.6.refs_2_.refs_4_
  87.8 2.9 %collective-permute-start.7 = (bf16[4,128,256]{2,1,0:T(8,128)(2,1)S(1)}, bf16[4,128,256]{2,1,0:T(8,128)(2,1)S(1)}, u32[]{:S(2)}, u32[]{:S(2)}) collective-permute-start(bf16[4,128,256]{2,1,0:T(8,128)(2,1)S(1)} %bitcast.16), channel_id=1, source_target_pairs={{0,64},{8,456},{16,80},{24,472},{32,96},{40,488},{48,112},{56,504}... | collective-permute-start | bytes 786440 | tf_op jit(solution)/shard_map/gather_keys_values/ppermute | solution.py:333
  90.8 2.3 %collective-permute-start.8 = (bf16[4,128,256]{2,1,0:T(8,128)(2,1)S(1)}, bf16[4,128,256]{2,1,0:T(8,128)(2,1)S(1)}, u32[]{:S(2)}, u32[]{:S(2)}) collective-permute-start(bf16[4,128,256]{2,1,0:T(8,128)(2,1)S(1)} %bitcast.17), channel_id=1, source_target_pairs={{0,32},{8,40},{16,48},{24,56},{32,64},{40,72},{48,80},{56,88},{64,... | collective-permute-start | bytes 786440 | tf_op jit(solution)/shard_map/gather_keys_values/ppermute | solution.py:333
  93.0 4.2 %collective-permute-start.9 = (bf16[4,128,256]{2,1,0:T(8,128)(2,1)S(1)}, bf16[4,128,256]{2,1,0:T(8,128)(2,1)S(1)}, u32[]{:S(2)}, u32[]{:S(2)}) collective-permute-start(bf16[4,128,256]{2,1,0:T(8,128)(2,1)S(1)} %bitcast.18), channel_id=1, source_target_pairs={{0,480},{8,488},{16,496},{24,504},{32,0},{40,8},{48,16},{56,24},{6... | collective-permute-start | bytes 786440 | tf_op jit(solution)/shard_map/gather_keys_values/ppermute | solution.py:333
  97.3 5.4 %attend.2 = (bf16[512,1024]{1,0:T(8,128)(2,1)S(1)}, f32[512,128]{1,0:T(8,128)S(1)}, bf16[8,512,256]{2,1,0:T(8,128)(2,1)S(1)}, s32[49]{0:T(128)S(1)}) custom-call(s32[24]{0:T(128)S(1)} %copy-done.2, s32[128]{0:T(128)S(1)} %copy-done.4, s32[2]{0:T(128)S(1)} %pad_add_fusion.place_ref, bf16[4,128,256]{2,1,0:T(8,128)(2,1)S(1)} %bitcast.19, ...), custom_call_target="tpu_custom_call" | custom-call | flops 2147483648 | bytes 2359296 | tf_op jit(solution)/shard_map/attend/pallas_call | solution.py:476
  102.7 0.0 collective-permute-done.7.refs_0_
  102.7 1.5 %collective-permute-done.8.refs_1_ = bf16[4,128,256]{2,1,0:T(8,128)(2,1)S(1)} collective-permute-done((bf16[4,128,256]{2,1,0:T(8,128)(2,1)S(1)}, bf16[4,128,256]{2,1,0:T(8,128)(2,1)S(1)}, u32[]{:S(2)}, u32[]{:S(2)}) %collective-permute-start.8) | collective-permute-done | bytes 262176 | tf_op jit(solution)/shard_map/gather_keys_values/ppermute | solution.py:333
  104.2 0.0 collective-permute-done.9.refs_2_
  104.2 1.0 attend.3
  105.2 8.7 %collective-permute-start.10 = (bf16[256,1152]{1,0:T(8,128)(2,1)S(1)}, bf16[256,1152]{1,0:T(8,128)(2,1)S(1)}, u32[]{:S(2)}, u32[]{:S(2)}) collective-permute-start(bf16[256,1152]{1,0:T(8,128)(2,1)S(1)} %get-tuple-element.30), channel_id=1, source_target_pairs={{0,8},{8,0},{16,24},{24,16},{32,40},{40,32},{48,56},{56,48},{64,72... | collective-permute-start | bytes 1769480 | tf_op jit(solution)/shard_map/attend/ppermute | solution.py:350
  113.9 1.6 %collective-permute-done.10.came_ref.core_ref = bf16[256,1152]{1,0:T(8,128)(2,1)S(1)} collective-permute-done((bf16[256,1152]{1,0:T(8,128)(2,1)S(1)}, bf16[256,1152]{1,0:T(8,128)(2,1)S(1)}, u32[]{:S(2)}, u32[]{:S(2)}) %collective-permute-start.10) | collective-permute-done | bytes 589856 | tf_op jit(solution)/shard_map/attend/ppermute | solution.py:350
  115.5 0.2 sum_attention.2
  115.7 3.4 %collective-permute-start.11 = (bf16[128,1152]{1,0:T(8,128)(2,1)S(1)}, bf16[128,1152]{1,0:T(8,128)(2,1)S(1)}, u32[]{:S(2)}, u32[]{:S(2)}) collective-permute-start(bf16[128,1152]{1,0:T(8,128)(2,1)S(1)} %sum_attention.2), channel_id=1, source_target_pairs={{0,16},{8,24},{16,0},{24,8},{32,48},{40,56},{48,32},{56,40},{64,80... | collective-permute-start | bytes 884744 | tf_op jit(solution)/shard_map/sum_attention/ppermute | solution.py:350
  119.8 7.6 %collective-permute-done.11.chip_ref = bf16[128,1152]{1,0:T(8,128)(2,1)S(1)} collective-permute-done((bf16[128,1152]{1,0:T(8,128)(2,1)S(1)}, bf16[128,1152]{1,0:T(8,128)(2,1)S(1)}, u32[]{:S(2)}, u32[]{:S(2)}) %collective-permute-start.11) | collective-permute-done | bytes 294944 | tf_op jit(solution)/shard_map/sum_attention/ppermute | solution.py:350
  127.4 1.6 %sum_attention.3 = bf16[128,1024]{1,0:T(8,128)(2,1)} custom-call(s32[24]{0:T(128)S(1)} %copy-done.2, s32[2]{0:T(128)S(1)} %pad_add_fusion.place_ref, f32[1,1]{1,0:T(1,128)} %bitcast.9.gate_ref, bf16[256,1152]{1,0:T(8,128)(2,1)S(1)} %get-tuple-element.29.kept_ref, bf16[256,1152]{1,0:T(8,128)(2,1)S(1)} %collective-permute-done.10.came_ref.core_ref, ...), custom_call_target="tpu_custom_call" | custom-call | tf_op jit(solution)/shard_map/sum_attention/pallas_call | solution.py:527
  (7 shorter events, 0.1 us)
Async XLA Ops:
  2.4 10.8 %copy-start = (bf16[128,1024]{1,0:T(8,128)(2,1)S(1)}, bf16[128,1024]{1,0:T(8,128)(2,1)}, u32[]{:S(2)}) copy-start(bf16[128,1024]{1,0:T(8,128)(2,1)} %q_ref.1) | copy-start | bytes 786436
  2.4 10.8 %copy-start.1 = (f32[128]{0:T(128)S(1)}, f32[128]{0:T(128)}, u32[]{:S(2)}) copy-start(f32[128]{0:T(128)} %param.10) | copy-start | bytes 1540
  2.4 13.2 %copy-start.5 = (bf16[128,128]{1,0:T(8,128)(2,1)S(1)}, bf16[128,128]{1,0:T(8,128)(2,1)}, u32[]{:S(2)}) copy-start(bf16[128,128]{1,0:T(8,128)(2,1)} %param.15) | copy-start | bytes 98308
  2.4 13.2 %copy-start.6 = (bf16[128,128]{1,0:T(8,128)(2,1)S(1)}, bf16[128,128]{1,0:T(8,128)(2,1)}, u32[]{:S(2)}) copy-start(bf16[128,128]{1,0:T(8,128)(2,1)} %param.14) | copy-start | bytes 98308
  2.4 45.7 %all-to-all-start = ((bf16[32,2,128,128]{3,2,1,0:T(8,128)(2,1)}), bf16[32,2,128,128]{3,2,1,0:T(8,128)(2,1)S(1)}, u32[]{:S(2)}, u32[]{:S(2)}) async-start(bf16[32,2,128,128]{3,2,1,0:T(8,128)(2,1)} %bitcast.22), calls=%async_computation | async-start | bytes 4194304 | tf_op jit(solution)/shard_map/spread_vision/all_to_all | solution.py:406
  13.4 34.7 %collective-permute-start = (bf16[8,128,128]{2,1,0:T(8,128)(2,1)S(1)}, bf16[8,128,128]{2,1,0:T(8,128)(2,1)S(1)}, u32[]{:S(2)}, u32[]{:S(2)}) collective-permute-start(bf16[8,128,128]{2,1,0:T(8,128)(2,1)S(1)} %norm_queries.1.refs_1_), channel_id=1, source_target_pairs={{0,8},{8,0},{16,24},{24,16},{32,40},{40,32},{48,56},{56,48},{64,72... | collective-permute-start | bytes 786440 | tf_op jit(solution)/shard_map/share_queries/ppermute | solution.py:350
  38.5 15.3 %collective-permute-start.3 = (bf16[4,128,256]{2,1,0:T(8,128)(2,1)S(1)}, bf16[4,128,256]{2,1,0:T(8,128)(2,1)}, u32[]{:S(2)}, u32[]{:S(2)}) collective-permute-start(bf16[4,128,256]{2,1,0:T(8,128)(2,1)S(1)} %bitcast.12), channel_id=1, source_target_pairs={{0,64},{8,456},{16,80},{24,472},{32,96},{40,488},{48,112},{56,504}... | collective-permute-start | bytes 786440 | tf_op jit(solution)/shard_map/gather_projections/ppermute | solution.py:333
  41.6 13.6 %collective-permute-start.1 = (bf16[4,128,256]{2,1,0:T(8,128)(2,1)S(1)}, bf16[4,128,256]{2,1,0:T(8,128)(2,1)S(1)}, u32[]{:S(2)}, u32[]{:S(2)}) collective-permute-start(bf16[4,128,256]{2,1,0:T(8,128)(2,1)S(1)} %bitcast.13), channel_id=1, source_target_pairs={{0,32},{8,40},{16,48},{24,56},{32,64},{40,72},{48,80},{56,88},{64,... | collective-permute-start | bytes 786440 | tf_op jit(solution)/shard_map/gather_projections/ppermute | solution.py:333
  44.6 10.6 %collective-permute-start.2 = (bf16[4,128,256]{2,1,0:T(8,128)(2,1)S(1)}, bf16[4,128,256]{2,1,0:T(8,128)(2,1)S(1)}, u32[]{:S(2)}, u32[]{:S(2)}) collective-permute-start(bf16[4,128,256]{2,1,0:T(8,128)(2,1)S(1)} %bitcast.14), channel_id=1, source_target_pairs={{0,480},{8,488},{16,496},{24,504},{32,0},{40,8},{48,16},{56,24},{6... | collective-permute-start | bytes 786440 | tf_op jit(solution)/shard_map/gather_projections/ppermute | solution.py:333
  48.9 38.9 %collective-permute-start.6 = (bf16[16,128,128]{2,1,0:T(8,128)(2,1)}, bf16[16,128,128]{2,1,0:T(8,128)(2,1)}, u32[]{:S(2)}, u32[]{:S(2)}) collective-permute-start(bf16[16,128,128]{2,1,0:T(8,128)(2,1)} %pad_maximum_fusion), channel_id=1, source_target_pairs={{0,16},{8,24},{16,0},{24,8},{32,48},{40,56},{48,32},{56,40},{64,80... | collective-permute-start | bytes 1572872 | tf_op jit(solution)/shard_map/share_queries/ppermute | solution.py:350
  55.1 15.9 %copy-start.3 = (f32[128]{0:T(128)S(1)}, f32[128]{0:T(128)}, u32[]{:S(2)}) copy-start(f32[128]{0:T(128)} %param.11) | copy-start | bytes 1540
  55.1 42.1 %copy-start.2 = (s32[24]{0:T(128)S(1)}, s32[24]{0:T(128)}, u32[]{:S(2)}) copy-start(s32[24]{0:T(128)} %image_start_ref.3) | copy-start | bytes 292
  55.2 42.1 %copy-start.4 = (s32[128]{0:T(128)S(1)}, s32[128]{0:T(128)}, u32[]{:S(2)}) copy-start(s32[128]{0:T(128)} %slot_image_ref.1) | copy-start | bytes 1540
  56.2 7.4 %collective-permute-start.4 = (bf16[256,384]{1,0:T(8,128)(2,1)S(1)}, bf16[256,384]{1,0:T(8,128)(2,1)S(1)}, u32[]{:S(2)}, u32[]{:S(2)}) collective-permute-start(bf16[256,384]{1,0:T(8,128)(2,1)S(1)} %get-tuple-element.20), channel_id=1, source_target_pairs={{0,8},{8,0},{16,24},{24,16},{32,40},{40,32},{48,56},{56,48},{64,72... | collective-permute-start | bytes 589832 | tf_op jit(solution)/shard_map/sum_projections/ppermute | solution.py:350
  63.6 7.4 %collective-permute-start.5 = (bf16[128,384]{1,0:T(8,128)(2,1)S(1)}, bf16[128,384]{1,0:T(8,128)(2,1)S(1)}, u32[]{:S(2)}, u32[]{:S(2)}) collective-permute-start(bf16[128,384]{1,0:T(8,128)(2,1)S(1)} %sum_projections.2), channel_id=1, source_target_pairs={{0,16},{8,24},{16,0},{24,8},{32,48},{40,56},{48,32},{56,40},{64,80... | collective-permute-start | bytes 294920 | tf_op jit(solution)/shard_map/sum_projections/ppermute | solution.py:350
  87.8 14.9 %collective-permute-start.7 = (bf16[4,128,256]{2,1,0:T(8,128)(2,1)S(1)}, bf16[4,128,256]{2,1,0:T(8,128)(2,1)S(1)}, u32[]{:S(2)}, u32[]{:S(2)}) collective-permute-start(bf16[4,128,256]{2,1,0:T(8,128)(2,1)S(1)} %bitcast.16), channel_id=1, source_target_pairs={{0,64},{8,456},{16,80},{24,472},{32,96},{40,488},{48,112},{56,504}... | collective-permute-start | bytes 786440 | tf_op jit(solution)/shard_map/gather_keys_values/ppermute | solution.py:333
  90.8 13.5 %collective-permute-start.8 = (bf16[4,128,256]{2,1,0:T(8,128)(2,1)S(1)}, bf16[4,128,256]{2,1,0:T(8,128)(2,1)S(1)}, u32[]{:S(2)}, u32[]{:S(2)}) collective-permute-start(bf16[4,128,256]{2,1,0:T(8,128)(2,1)S(1)} %bitcast.17), channel_id=1, source_target_pairs={{0,32},{8,40},{16,48},{24,56},{32,64},{40,72},{48,80},{56,88},{64,... | collective-permute-start | bytes 786440 | tf_op jit(solution)/shard_map/gather_keys_values/ppermute | solution.py:333
  93.0 11.2 %collective-permute-start.9 = (bf16[4,128,256]{2,1,0:T(8,128)(2,1)S(1)}, bf16[4,128,256]{2,1,0:T(8,128)(2,1)S(1)}, u32[]{:S(2)}, u32[]{:S(2)}) collective-permute-start(bf16[4,128,256]{2,1,0:T(8,128)(2,1)S(1)} %bitcast.18), channel_id=1, source_target_pairs={{0,480},{8,488},{16,496},{24,504},{32,0},{40,8},{48,16},{56,24},{6... | collective-permute-start | bytes 786440 | tf_op jit(solution)/shard_map/gather_keys_values/ppermute | solution.py:333
  105.2 10.3 %collective-permute-start.10 = (bf16[256,1152]{1,0:T(8,128)(2,1)S(1)}, bf16[256,1152]{1,0:T(8,128)(2,1)S(1)}, u32[]{:S(2)}, u32[]{:S(2)}) collective-permute-start(bf16[256,1152]{1,0:T(8,128)(2,1)S(1)} %get-tuple-element.30), channel_id=1, source_target_pairs={{0,8},{8,0},{16,24},{24,16},{32,40},{40,32},{48,56},{56,48},{64,72... | collective-permute-start | bytes 1769480 | tf_op jit(solution)/shard_map/attend/ppermute | solution.py:350
  115.7 11.6 %collective-permute-start.11 = (bf16[128,1152]{1,0:T(8,128)(2,1)S(1)}, bf16[128,1152]{1,0:T(8,128)(2,1)S(1)}, u32[]{:S(2)}, u32[]{:S(2)}) collective-permute-start(bf16[128,1152]{1,0:T(8,128)(2,1)S(1)} %sum_attention.2), channel_id=1, source_target_pairs={{0,16},{8,24},{16,0},{24,8},{32,48},{40,56},{48,32},{56,40},{64,80... | collective-permute-start | bytes 884744 | tf_op jit(solution)/shard_map/sum_attention/ppermute | solution.py:350

commit v2 on v1

--- a/solution.py
+++ b/solution.py
@@ -11,6 +11,7 @@
 EPS = 1e-05
 PLANE = 4
 VMEM_LIMIT = 16 * 1024 * 1024
+TOKEN_ORDER = (0, 2, 1, 3)
 SPREAD_LIMIT = 62 * 1024 * 1024
 NO_IMAGE = 127
 HIDE = -30000.0
@@ -198,7 +199,8 @@
     starts = jnp.full((own, head_dim), total_tokens, jnp.int32)
     for image in range(n_images):
         starts = jnp.where(lane == image, image_start_ref[image], starts)
-    for at, one in enumerate(order_of(member)):
+    for at, mask in enumerate(TOKEN_ORDER):
+        one = member ^ mask
         position = (
             first_token + one * own + lax.broadcasted_iota(jnp.int32, (own, head_dim), 0)
         )
@@ -229,62 +231,85 @@
     lax.fori_loop(0, heads, one_head, 0, unroll=2)
 
 
-def attend_last_kernel(plan_ref, *refs, scale, group, slots_here):
-    sources = SOURCES[1:]
-    kv_refs = refs[: len(sources)]
-    numer_ref, came_ref, marked_ref, kept_ref, to_core_ref = refs[len(sources) : -3]
-    keys_ref, values_ref, sums_ref = refs[-3:]
-    heads, tokens, width = marked_ref.shape
-    head_dim = width // 2
-
+def pack_slots(plan_ref, kv_refs, keys_ref, values_ref, group, slots_here):
     put = functools.partial(put_slot, keys_ref, values_ref)
     number = 0
-    for kv_ref, (_, several) in zip(kv_refs, sources):
+    for kv_ref, (_, several) in zip(kv_refs, SOURCES[1:]):
         for at in range(len(several)):
             for here in range(slots_here):
                 image, to = plan_ref[2 * number], plan_ref[2 * number + 1]
                 pl.when(to >= 0)(functools.partial(put, to, kv_ref, at, here, image))
                 number += 1
     kept = plan_ref[2 * number]
-    turns = (kept + group - 1) // group
 
     def fill(to, _):
         put(to, kv_refs[0], 0, 0, NO_IMAGE)
         return 0
 
-    lax.fori_loop(kept, turns * group, fill, 0)
-    sums_ref[...] = came_ref[...]
+    lax.fori_loop(kept, (kept + group - 1) // group * group, fill, 0)
+
+
+def attend_last_kernel(plan_ref, *refs, scale, group, slots_here, pack, first, together):
+    numer_ref, came_ref, marked_ref = refs[:3]
+    if pack:
+        kv_refs, refs = refs[3 : 2 + len(SOURCES)], refs[2 + len(SOURCES) :]
+        out_refs, (keys_ref, values_ref, sums_ref) = refs[:-3], refs[-3:]
+        pack_slots(plan_ref, kv_refs, keys_ref, values_ref, group, slots_here)
+    else:
+        keys_ref, values_ref, *out_refs, sums_ref = refs[3:]
+    heads, _, width = marked_ref.shape
+    head_dim = width // 2
+    count = sums_ref.shape[0]
+    rows = slice(first, first + count)
+    slots = keys_ref.shape[0]
+    kept = plan_ref[2 * slots]
+    turns = (kept + group - 1) // group
+    sums_ref[...] = came_ref[rows]
     column = lax.broadcasted_iota(jnp.int32, sums_ref.shape, 1)
-    half = tokens // 2
-
-    def one_head(head, _, count):
-        keys = keys_ref[:count].reshape(-1, 2 * head_dim)
-        values = values_ref[:count].reshape(-1, 2 * head_dim)
-        total = weigh(marked_ref[head], keys, values, scale)
-        at = pl.ds(pl.multiple_of(head * head_dim, head_dim), head_dim)
-        numer = (numer_ref[:, at].astype(jnp.float32) + total[:, :head_dim]).astype(jnp.bfloat16)
-        kept_ref[:, at] = numer[:half]
-        to_core_ref[:, at] = numer[half:]
+
+    def store(at, values):
+        start = 0
+        for out_ref in out_refs:
+            stop = start + out_ref.shape[0]
+            out_ref[:, at] = values[start:stop]
+            start = stop
+
+    def some_heads(number, _, packed):
+        keys = keys_ref[:packed].reshape(-1, width)
+        values = values_ref[:packed].reshape(-1, width)
+        several = [number * together + i for i in range(together)]
+        queries = jnp.concatenate([marked_ref[head, rows] for head in several], axis=0)
+        totals = weigh(queries, keys, values, scale)
         sums = sums_ref[...]
-        sums_ref[...] = jnp.where(column == head, sums + total[:, head_dim:], sums)
+        for i, head in enumerate(several):
+            total = totals[count * i : count * (i + 1)]
+            at = pl.ds(pl.multiple_of(head * head_dim, head_dim), head_dim)
+            numer = numer_ref[rows, at].astype(jnp.float32) + total[:, :head_dim]
+            store(at, numer.astype(jnp.bfloat16))
+            sums = jnp.where(column == head, sums + total[:, head_dim:], sums)
+        sums_ref[...] = sums
         return 0
 
-    for turn in range(1, keys_ref.shape[0] // group + 1):
+    for turn in range(1, slots // group + 1):
 
         @pl.when(turns == turn)
         def _():
             lax.fori_loop(
-                0, heads, functools.partial(one_head, count=turn * group), 0, unroll=2
+                0,
+                heads // together,
+                functools.partial(some_heads, packed=turn * group),
+                0,
+                unroll=2,
             )
 
     @pl.when(turns == 0)
     def _():
-        kept_ref[:, : heads * head_dim] = numer_ref[:half]
-        to_core_ref[:, : heads * head_dim] = numer_ref[half:]
-
-    sums = split_sums(sums_ref[...], heads).astype(jnp.bfloat16)
-    kept_ref[:, heads * head_dim :] = sums[:half]
-    to_core_ref[:, heads * head_dim :] = sums[half:]
+        store(slice(0, heads * head_dim), numer_ref[rows])
+
+    store(
+        slice(heads * head_dim, (heads + 1) * head_dim),
+        split_sums(sums_ref[...], heads).astype(jnp.bfloat16),
+    )
 
 
 def add_kernel(kept_ref, came_ref, out_ref, *, heads):
@@ -293,10 +318,10 @@
     for first in range(0, cut, 256):
         columns = slice(first, min(first + 256, cut))
         out_ref[:, columns] = (
-            kept_ref[own:, columns].astype(jnp.float32)
+            kept_ref[:, columns].astype(jnp.float32)
             + came_ref[own:, columns].astype(jnp.float32)
         ).astype(out_ref.dtype)
-    sums = kept_ref[own:, cut:].astype(jnp.float32) + came_ref[own:, cut:].astype(jnp.float32)
+    sums = kept_ref[:, cut:].astype(jnp.float32) + came_ref[own:, cut:].astype(jnp.float32)
     out_ref[:, cut:] = split_sums(join_sums(sums, heads), heads).astype(out_ref.dtype)
 
 
@@ -312,7 +337,7 @@
 
     def total(columns):
         return (
-            kept_ref[:own, columns].astype(jnp.float32)
+            kept_ref[:, columns].astype(jnp.float32)
             + core_ref[:own, columns].astype(jnp.float32)
             + chip_ref[:, columns].astype(jnp.float32)
         )
@@ -498,39 +523,57 @@
             all_kv[0],
             *(source for source, _ in plane_queries),
         )
-        own_and_chip, to_core = pl.pallas_call(
-            functools.partial(
-                attend_last_kernel, scale=scale, group=group, slots_here=slots_here
-            ),
-            out_shape=[jax.ShapeDtypeStruct((2 * tokens, width), jnp.bfloat16)] * 2,
-            in_specs=[smem()] + [vmem()] * (len(all_kv) - 1 + 3),
-            out_specs=[vmem()] * 2,
-            scratch_shapes=[
-                pltpu.VMEM((last_slots, tile_rows, 2 * head_dim), jnp.bfloat16),
-                pltpu.VMEM((last_slots, tile_rows, 2 * head_dim), jnp.bfloat16),
-                pltpu.VMEM((PLANE * tokens, head_dim), jnp.float32),
-            ],
-            compiler_params=params(),
-            cost_estimate=cost(PLANE * tokens, last_slots),
-        )(plan, *all_kv[1:], numer, sums, marked)
+        block = jax.ShapeDtypeStruct((tokens, width), jnp.bfloat16)
+        two_blocks = jax.ShapeDtypeStruct((2 * tokens, width), jnp.bfloat16)
+        packed = jax.ShapeDtypeStruct((last_slots, tile_rows, 2 * head_dim), jnp.bfloat16)
+
+        def attend_last(first, last, inputs, outputs, pack, together):
+            return pl.pallas_call(
+                functools.partial(
+                    attend_last_kernel,
+                    scale=scale,
+                    group=group,
+                    slots_here=slots_here,
+                    pack=pack,
+                    first=first * tokens,
+                    together=together,
+                ),
+                out_shape=outputs,
+                in_specs=[smem()] + [vmem()] * len(inputs),
+                out_specs=[vmem()] * len(outputs),
+                scratch_shapes=[pltpu.VMEM(((last - first) * tokens, head_dim), jnp.float32)],
+                compiler_params=params(),
+                cost_estimate=cost((last - first) * tokens, last_slots),
+            )(plan, *inputs)
+
+        to_chip, to_core, keys, values = attend_last(
+            1,
+            PLANE,
+            (numer, sums, marked, *all_kv[1:]),
+            [block, two_blocks, packed, packed],
+            True,
+            2,
+        )
+
+    with jax.named_scope("sum_attention"):
         from_core = other_member(to_core, 1)
-
-    with jax.named_scope("sum_attention"):
         to_chip = pl.pallas_call(
             functools.partial(add_kernel, heads=heads),
-            out_shape=jax.ShapeDtypeStruct((tokens, width), jnp.bfloat16),
+            out_shape=block,
             in_specs=[vmem(), vmem()],
             out_specs=vmem(),
             compiler_params=params(),
-        )(own_and_chip, from_core)
+        )(to_chip, from_core)
+        to_chip, keys = lax.optimization_barrier((to_chip, keys))
         from_chip = other_member(to_chip, 2)
+        [kept] = attend_last(0, 1, (numer, sums, marked, keys, values), [block], False, 4)
         return pl.pallas_call(
             combine_kernel,
             out_shape=jax.ShapeDtypeStruct((tokens, q_cols), jnp.bfloat16),
             in_specs=[smem(), smem()] + [vmem()] * 4,
             out_specs=vmem(),
             compiler_params=params(),
-        )(image_start, place, attn_gate.reshape(1, 1), own_and_chip, from_core, from_chip)
+        )(image_start, place, attn_gate.reshape(1, 1), kept, from_core, from_chip)
 
 
 def solution(mesh):

time: 130 us -> 129 us (level)
  Pallas kernels: 13.3 us -> 16.5 us
  starting transfers between devices: 59.1 us -> 56.3 us
  waiting for transfers between devices: 15.1 us -> 13.7 us
    pallas_call x2 -> x3, Pallas kernels: 1.21 us -> 4.4 us  [the longest x2 4.18 us: attend_last(): pl.pallas_call(functools.partial(attend_last_kernel, scale=scale, group=g...]
    ppermute x6, starting transfers between devices: 29.4 us -> 26.6 us  [other_member(): return lax.ppermute(value, 'ctx', [(i, i ^ mask) for i in range(ctx_size)])]
    ppermute x6, waiting for transfers between devices: 13.6 us -> 12.2 us  [other_member(): return lax.ppermute(value, 'ctx', [(i, i ^ mask) for i in range(ctx_size)])]
  transfers between devices with their start and end apart: 13 -> 13, of which waited for: 5 -> 5; matrix products, arithmetic and copies ran while one was open for 1% -> 1% of each run, Pallas kernels for 6% -> 7%
where the time goes in v2:
time: 129 us; the launch traced here: 128 us
  starting transfers between devices  56.3 us (44%)
  blocking collectives  39.5 us (31%)
  Pallas kernels  16.5 us (13%)
  waiting for transfers between devices  13.7 us (11%)
    all_gather x2, blocking collectives, gather_along_z(): own = lax.all_gather(block, 'ctx', axis_index_groups=groups)  39.5 us
    ppermute x6, starting transfers between devices, other_member(): return lax.ppermute(value, 'ctx', [(i, i ^ mask) for i in range(ctx_size)])  26.6 us
    ppermute x6, starting transfers between devices, shift(): lax.ppermute(value, 'ctx', [(i, (i + moves[i]) % ctx_size) for i in range...  19 us
    ppermute x6, waiting for transfers between devices, other_member(): return lax.ppermute(value, 'ctx', [(i, i ^ mask) for i in range(ctx_size)])  12.2 us
    all_to_all x1, starting transfers between devices, local(): lax.all_to_all(mine, ('ctx', 'head'), 0, 0, axis_index_groups=whole_plane)  10.7 us
    pallas_call x1, Pallas kernels, local(): pl.pallas_call(functools.partial(attend_first_kernel, scale=scale, slots_...  5.44 us
    pallas_call x2, Pallas kernels, attend_last(): pl.pallas_call(functools.partial(attend_last_kernel, scale=scale, group=g...  4.18 us
  transfers between devices with their start and end apart: 13, of which 5 were waited for; matrix products, arithmetic and copies ran while one was open for 1% of the time, Pallas kernels for 7%

profile of v2, /device:TPU:1, one launch (start us, length us, event | category | flops | bytes accessed | tf_op | source)
XLA Modules:
  0.0 128.0 jit_solution(5018357802454952448)
XLA Ops:
  0.0 2.4 %spread_vision.1 = bf16[4,8,2,128,128]{4,3,2,1,0:T(8,128)(2,1)} custom-call(bf16[128,1024]{1,0:T(8,128)(2,1)} %x_ref.1), custom_call_target="tpu_custom_call" | custom-call | tf_op jit(solution)/shard_map/spread_vision/pallas_call | solution.py:417
  2.4 0.0 copy-start
  2.4 0.0 copy-start.1
  2.4 0.0 copy-start.5
  2.4 0.0 copy-start.6
  2.4 10.7 %all-to-all-start = ((bf16[32,2,128,128]{3,2,1,0:T(8,128)(2,1)}), bf16[32,2,128,128]{3,2,1,0:T(8,128)(2,1)S(1)}, u32[]{:S(2)}, u32[]{:S(2)}) async-start(bf16[32,2,128,128]{3,2,1,0:T(8,128)(2,1)} %bitcast.22), calls=%async_computation | async-start | bytes 4194304 | tf_op jit(solution)/shard_map/spread_vision/all_to_all | solution.py:431
  13.2 0.0 copy-done
  13.2 0.2 norm_queries.1.refs_1_
  13.4 2.2 %collective-permute-start = (bf16[8,128,128]{2,1,0:T(8,128)(2,1)S(1)}, bf16[8,128,128]{2,1,0:T(8,128)(2,1)S(1)}, u32[]{:S(2)}, u32[]{:S(2)}) collective-permute-start(bf16[8,128,128]{2,1,0:T(8,128)(2,1)S(1)} %norm_queries.1.refs_1_), channel_id=1, source_target_pairs={{0,8},{8,0},{16,24},{24,16},{32,40},{40,32},{48,56},{56,48},{64,72... | collective-permute-start | bytes 786440 | tf_op jit(solution)/shard_map/share_queries/ppermute | solution.py:375
  15.7 22.8 %all-gather = bf16[512,256]{1,0:T(8,128)(2,1)S(1)} all-gather(bf16[128,256]{1,0:T(8,128)(2,1)S(1)} %pad_maximum_fusion.1), channel_id=2, replica_groups={{0,128,256,384},{32,160,288,416},{64,192,320,448},{96,224,352,480},{8,1..., dimensions={0}, use_global_device_ids=true | all-gather | bytes 327680 | tf_op jit(solution)/shard_map/gather_projections/all_gather | solution.py:367
  38.5 3.1 %collective-permute-start.3 = (bf16[4,128,256]{2,1,0:T(8,128)(2,1)S(1)}, bf16[4,128,256]{2,1,0:T(8,128)(2,1)}, u32[]{:S(2)}, u32[]{:S(2)}) collective-permute-start(bf16[4,128,256]{2,1,0:T(8,128)(2,1)S(1)} %bitcast.12), channel_id=1, source_target_pairs={{0,64},{8,456},{16,80},{24,472},{32,96},{40,488},{48,112},{56,504}... | collective-permute-start | bytes 786440 | tf_op jit(solution)/shard_map/gather_projections/ppermute | solution.py:358
  41.6 3.0 %collective-permute-start.1 = (bf16[4,128,256]{2,1,0:T(8,128)(2,1)S(1)}, bf16[4,128,256]{2,1,0:T(8,128)(2,1)S(1)}, u32[]{:S(2)}, u32[]{:S(2)}) collective-permute-start(bf16[4,128,256]{2,1,0:T(8,128)(2,1)S(1)} %bitcast.13), channel_id=1, source_target_pairs={{0,32},{8,40},{16,48},{24,56},{32,64},{40,72},{48,80},{56,88},{64,... | collective-permute-start | bytes 786440 | tf_op jit(solution)/shard_map/gather_projections/ppermute | solution.py:358
  44.6 3.5 %collective-permute-start.2 = (bf16[4,128,256]{2,1,0:T(8,128)(2,1)S(1)}, bf16[4,128,256]{2,1,0:T(8,128)(2,1)S(1)}, u32[]{:S(2)}, u32[]{:S(2)}) collective-permute-start(bf16[4,128,256]{2,1,0:T(8,128)(2,1)S(1)} %bitcast.14), channel_id=1, source_target_pairs={{0,480},{8,488},{16,496},{24,504},{32,0},{40,8},{48,16},{56,24},{6... | collective-permute-start | bytes 786440 | tf_op jit(solution)/shard_map/gather_projections/ppermute | solution.py:358
  48.1 0.0 collective-permute-done.refs_3_
  48.1 0.0 all-to-all-done
  48.1 0.8 pad_maximum_fusion
  48.9 4.7 %collective-permute-start.6 = (bf16[16,128,128]{2,1,0:T(8,128)(2,1)}, bf16[16,128,128]{2,1,0:T(8,128)(2,1)}, u32[]{:S(2)}, u32[]{:S(2)}) collective-permute-start(bf16[16,128,128]{2,1,0:T(8,128)(2,1)} %pad_maximum_fusion), channel_id=1, source_target_pairs={{0,16},{8,24},{16,0},{24,8},{32,48},{40,56},{48,32},{56,40},{64,80... | collective-permute-start | bytes 1572872 | tf_op jit(solution)/shard_map/share_queries/ppermute | solution.py:375
  53.7 0.1 pad_add_fusion.place_ref
  53.7 0.0 collective-permute-done.3.refs_1_
  53.7 1.4 %project.2.refs_2_ = f32[512,256]{1,0:T(8,128)S(1)} custom-call(s32[2]{0:T(128)S(1)} %pad_add_fusion.place_ref, bf16[4,16,128,128]{3,2,1,0:T(8,128)(2,1)S(1)} %bitcast.10, bf16[4,128,256]{2,1,0:T(8,128)(2,1)S(1)} %bitcast.15, bf16[4,128,256]{2,1,0:T(8,128)(2,1)} %collective-permute-done.3.refs_1_), custom_call_target="tpu_custom_call" | custom-call | tf_op jit(solution)/shard_map/project/pallas_call | solution.py:445
  55.1 0.0 copy-start.3
  55.1 0.0 copy-start.2
  55.2 0.0 copy-start.4
  55.2 0.0 collective-permute-done.1.refs_0_
  55.2 0.0 collective-permute-done.2.refs_1_
  55.2 1.0 project.3
  56.2 6.3 %collective-permute-start.4 = (bf16[256,384]{1,0:T(8,128)(2,1)S(1)}, bf16[256,384]{1,0:T(8,128)(2,1)S(1)}, u32[]{:S(2)}, u32[]{:S(2)}) collective-permute-start(bf16[256,384]{1,0:T(8,128)(2,1)S(1)} %get-tuple-element.24), channel_id=1, source_target_pairs={{0,8},{8,0},{16,24},{24,16},{32,40},{40,32},{48,56},{56,48},{64,72... | collective-permute-start | bytes 589832 | tf_op jit(solution)/shard_map/sum_projections/ppermute | solution.py:375
  62.5 1.0 collective-permute-done.4.came_ref.core_ref
  63.6 4.1 %collective-permute-start.5 = (bf16[128,384]{1,0:T(8,128)(2,1)S(1)}, bf16[128,384]{1,0:T(8,128)(2,1)S(1)}, u32[]{:S(2)}, u32[]{:S(2)}) collective-permute-start(bf16[128,384]{1,0:T(8,128)(2,1)S(1)} %sum_projections.2), channel_id=1, source_target_pairs={{0,16},{8,24},{16,0},{24,8},{32,48},{40,56},{48,32},{56,40},{64,80... | collective-permute-start | bytes 294920 | tf_op jit(solution)/shard_map/sum_projections/ppermute | solution.py:375
  67.7 3.3 %collective-permute-done.5.chip_ref = bf16[128,384]{1,0:T(8,128)(2,1)S(1)} collective-permute-done((bf16[128,384]{1,0:T(8,128)(2,1)S(1)}, bf16[128,384]{1,0:T(8,128)(2,1)S(1)}, u32[]{:S(2)}, u32[]{:S(2)}) %collective-permute-start.5) | collective-permute-done | bytes 98336 | tf_op jit(solution)/shard_map/sum_projections/ppermute | solution.py:375
  71.0 0.1 sum_projections.3
  71.1 16.7 %all-gather.1 = bf16[512,256]{1,0:T(8,128)(2,1)S(1)} all-gather(bf16[128,256]{1,0:T(8,128)(2,1)S(1)} %sum_projections.3), channel_id=3, replica_groups={{0,128,256,384},{32,160,288,416},{64,192,320,448},{96,224,352,480},{8,1..., dimensions={0}, use_global_device_ids=true | all-gather | bytes 327680 | tf_op jit(solution)/shard_map/gather_keys_values/all_gather | solution.py:367
  87.8 0.0 collective-permute-done.6.refs_2_.refs_4_
  87.8 2.9 %collective-permute-start.7 = (bf16[4,128,256]{2,1,0:T(8,128)(2,1)S(1)}, bf16[4,128,256]{2,1,0:T(8,128)(2,1)S(1)}, u32[]{:S(2)}, u32[]{:S(2)}) collective-permute-start(bf16[4,128,256]{2,1,0:T(8,128)(2,1)S(1)} %bitcast.16), channel_id=1, source_target_pairs={{0,64},{8,456},{16,80},{24,472},{32,96},{40,488},{48,112},{56,504}... | collective-permute-start | bytes 786440 | tf_op jit(solution)/shard_map/gather_keys_values/ppermute | solution.py:358
  90.8 2.3 %collective-permute-start.8 = (bf16[4,128,256]{2,1,0:T(8,128)(2,1)S(1)}, bf16[4,128,256]{2,1,0:T(8,128)(2,1)S(1)}, u32[]{:S(2)}, u32[]{:S(2)}) collective-permute-start(bf16[4,128,256]{2,1,0:T(8,128)(2,1)S(1)} %bitcast.17), channel_id=1, source_target_pairs={{0,32},{8,40},{16,48},{24,56},{32,64},{40,72},{48,80},{56,88},{64,... | collective-permute-start | bytes 786440 | tf_op jit(solution)/shard_map/gather_keys_values/ppermute | solution.py:358
  93.0 4.2 %collective-permute-start.9 = (bf16[4,128,256]{2,1,0:T(8,128)(2,1)S(1)}, bf16[4,128,256]{2,1,0:T(8,128)(2,1)S(1)}, u32[]{:S(2)}, u32[]{:S(2)}) collective-permute-start(bf16[4,128,256]{2,1,0:T(8,128)(2,1)S(1)} %bitcast.18), channel_id=1, source_target_pairs={{0,480},{8,488},{16,496},{24,504},{32,0},{40,8},{48,16},{56,24},{6... | collective-permute-start | bytes 786440 | tf_op jit(solution)/shard_map/gather_keys_values/ppermute | solution.py:358
  97.3 5.4 %attend.2 = (bf16[512,1024]{1,0:T(8,128)(2,1)S(1)}, f32[512,128]{1,0:T(8,128)S(1)}, bf16[8,512,256]{2,1,0:T(8,128)(2,1)S(1)}, s32[49]{0:T(128)S(1)}) custom-call(s32[24]{0:T(128)S(1)} %copy-done.2, s32[128]{0:T(128)S(1)} %copy-done.4, s32[2]{0:T(128)S(1)} %pad_add_fusion.place_ref, bf16[4,128,256]{2,1,0:T(8,128)(2,1)S(1)} %bitcast.19, ...), custom_call_target="tpu_custom_call" | custom-call | flops 2147483648 | bytes 2359296 | tf_op jit(solution)/shard_map/attend/pallas_call | solution.py:501
  102.7 0.0 collective-permute-done.7.refs_3_
  102.7 1.5 %collective-permute-done.8.refs_4_ = bf16[4,128,256]{2,1,0:T(8,128)(2,1)S(1)} collective-permute-done((bf16[4,128,256]{2,1,0:T(8,128)(2,1)S(1)}, bf16[4,128,256]{2,1,0:T(8,128)(2,1)S(1)}, u32[]{:S(2)}, u32[]{:S(2)}) %collective-permute-start.8) | collective-permute-done | bytes 262176 | tf_op jit(solution)/shard_map/gather_keys_values/ppermute | solution.py:358
  104.2 0.0 collective-permute-done.9.refs_5_
  104.2 2.8 %attend.3 = (bf16[128,1152]{1,0:T(8,128)(2,1)S(1)}, bf16[256,1152]{1,0:T(8,128)(2,1)S(1)}, bf16[24,64,256]{2,1,0:T(8,128)(2,1)S(1)}, bf16[24,64,256]{2,1,0:T(8,128)(2,1)S(1)}) custom-call(s32[49]{0:T(128)S(1)} %get-tuple-element.29.plan_ref, bf16[512,1024]{1,0:T(8,128)(2,1)S(1)} %get-tuple-element.30.refs_0_, f32[512,128]{1,0:T(8,128)S(1)} %get-tuple-element.31.refs_1_, ...), custom_call_target="tpu_custom_call" | custom-call | flops 4831838208 | bytes 1769472 | tf_op jit(solution)/shard_map/attend/pallas_call | solution.py:531
  107.0 5.9 %collective-permute-start.10 = (bf16[256,1152]{1,0:T(8,128)(2,1)S(1)}, bf16[256,1152]{1,0:T(8,128)(2,1)S(1)}, u32[]{:S(2)}, u32[]{:S(2)}) collective-permute-start(bf16[256,1152]{1,0:T(8,128)(2,1)S(1)} %get-tuple-element.34), channel_id=1, source_target_pairs={{0,8},{8,0},{16,24},{24,16},{32,40},{40,32},{48,56},{56,48},{64,72... | collective-permute-start | bytes 1769480 | tf_op jit(solution)/shard_map/sum_attention/ppermute | solution.py:375
  112.9 1.6 %collective-permute-done.10.came_ref.core_ref = bf16[256,1152]{1,0:T(8,128)(2,1)S(1)} collective-permute-done((bf16[256,1152]{1,0:T(8,128)(2,1)S(1)}, bf16[256,1152]{1,0:T(8,128)(2,1)S(1)}, u32[]{:S(2)}, u32[]{:S(2)}) %collective-permute-start.10) | collective-permute-done | bytes 589856 | tf_op jit(solution)/shard_map/sum_attention/ppermute | solution.py:375
  114.6 0.2 sum_attention.3
  114.8 3.4 %collective-permute-start.11 = (bf16[128,1152]{1,0:T(8,128)(2,1)S(1)}, bf16[128,1152]{1,0:T(8,128)(2,1)S(1)}, u32[]{:S(2)}, u32[]{:S(2)}) collective-permute-start(bf16[128,1152]{1,0:T(8,128)(2,1)S(1)} %sum_attention.3), channel_id=1, source_target_pairs={{0,16},{8,24},{16,0},{24,8},{32,48},{40,56},{48,32},{56,40},{64,80... | collective-permute-start | bytes 884744 | tf_op jit(solution)/shard_map/sum_attention/ppermute | solution.py:375
  118.8 1.4 %sum_attention.4.kept_ref = bf16[128,1152]{1,0:T(8,128)(2,1)S(1)} custom-call(s32[49]{0:T(128)S(1)} %get-tuple-element.29.plan_ref, bf16[512,1024]{1,0:T(8,128)(2,1)S(1)} %get-tuple-element.30.refs_0_, f32[512,128]{1,0:T(8,128)S(1)} %get-tuple-element.31.refs_1_, bf16[8,512,256]{2,1,0:T(8,128)(2,1)S(1)} %get-tuple-element.32.refs_2_, ...), custom_call_target="tpu_custom_call" | custom-call | flops 1610612736 | bytes 589824 | tf_op jit(solution)/shard_map/sum_attention/pallas_call | solution.py:531
  120.2 6.2 %collective-permute-done.11.chip_ref = bf16[128,1152]{1,0:T(8,128)(2,1)S(1)} collective-permute-done((bf16[128,1152]{1,0:T(8,128)(2,1)S(1)}, bf16[128,1152]{1,0:T(8,128)(2,1)S(1)}, u32[]{:S(2)}, u32[]{:S(2)}) %collective-permute-start.11) | collective-permute-done | bytes 294944 | tf_op jit(solution)/shard_map/sum_attention/ppermute | solution.py:375
  126.4 1.6 %sum_attention.5 = bf16[128,1024]{1,0:T(8,128)(2,1)} custom-call(s32[24]{0:T(128)S(1)} %copy-done.2, s32[2]{0:T(128)S(1)} %pad_add_fusion.place_ref, f32[1,1]{1,0:T(1,128)} %bitcast.9.gate_ref, bf16[128,1152]{1,0:T(8,128)(2,1)S(1)} %sum_attention.4.kept_ref, bf16[256,1152]{1,0:T(8,128)(2,1)S(1)} %collective-permute-done.10.came_ref.core_ref, ...), custom_call_target="tpu_custom_call" | custom-call | tf_op jit(solution)/shard_map/sum_attention/pallas_call | solution.py:570
  (8 shorter events, 0.1 us)
Async XLA Ops:
  2.4 10.8 %copy-start = (bf16[128,1024]{1,0:T(8,128)(2,1)S(1)}, bf16[128,1024]{1,0:T(8,128)(2,1)}, u32[]{:S(2)}) copy-start(bf16[128,1024]{1,0:T(8,128)(2,1)} %q_ref.1) | copy-start | bytes 786436
  2.4 10.8 %copy-start.1 = (f32[128]{0:T(128)S(1)}, f32[128]{0:T(128)}, u32[]{:S(2)}) copy-start(f32[128]{0:T(128)} %param.10) | copy-start | bytes 1540
  2.4 13.2 %copy-start.5 = (bf16[128,128]{1,0:T(8,128)(2,1)S(1)}, bf16[128,128]{1,0:T(8,128)(2,1)}, u32[]{:S(2)}) copy-start(bf16[128,128]{1,0:T(8,128)(2,1)} %param.15) | copy-start | bytes 98308
  2.4 13.2 %copy-start.6 = (bf16[128,128]{1,0:T(8,128)(2,1)S(1)}, bf16[128,128]{1,0:T(8,128)(2,1)}, u32[]{:S(2)}) copy-start(bf16[128,128]{1,0:T(8,128)(2,1)} %param.14) | copy-start | bytes 98308
  2.4 45.7 %all-to-all-start = ((bf16[32,2,128,128]{3,2,1,0:T(8,128)(2,1)}), bf16[32,2,128,128]{3,2,1,0:T(8,128)(2,1)S(1)}, u32[]{:S(2)}, u32[]{:S(2)}) async-start(bf16[32,2,128,128]{3,2,1,0:T(8,128)(2,1)} %bitcast.22), calls=%async_computation | async-start | bytes 4194304 | tf_op jit(solution)/shard_map/spread_vision/all_to_all | solution.py:431
  13.4 34.7 %collective-permute-start = (bf16[8,128,128]{2,1,0:T(8,128)(2,1)S(1)}, bf16[8,128,128]{2,1,0:T(8,128)(2,1)S(1)}, u32[]{:S(2)}, u32[]{:S(2)}) collective-permute-start(bf16[8,128,128]{2,1,0:T(8,128)(2,1)S(1)} %norm_queries.1.refs_1_), channel_id=1, source_target_pairs={{0,8},{8,0},{16,24},{24,16},{32,40},{40,32},{48,56},{56,48},{64,72... | collective-permute-start | bytes 786440 | tf_op jit(solution)/shard_map/share_queries/ppermute | solution.py:375
  38.5 15.3 %collective-permute-start.3 = (bf16[4,128,256]{2,1,0:T(8,128)(2,1)S(1)}, bf16[4,128,256]{2,1,0:T(8,128)(2,1)}, u32[]{:S(2)}, u32[]{:S(2)}) collective-permute-start(bf16[4,128,256]{2,1,0:T(8,128)(2,1)S(1)} %bitcast.12), channel_id=1, source_target_pairs={{0,64},{8,456},{16,80},{24,472},{32,96},{40,488},{48,112},{56,504}... | collective-permute-start | bytes 786440 | tf_op jit(solution)/shard_map/gather_projections/ppermute | solution.py:358
  41.6 13.6 %collective-permute-start.1 = (bf16[4,128,256]{2,1,0:T(8,128)(2,1)S(1)}, bf16[4,128,256]{2,1,0:T(8,128)(2,1)S(1)}, u32[]{:S(2)}, u32[]{:S(2)}) collective-permute-start(bf16[4,128,256]{2,1,0:T(8,128)(2,1)S(1)} %bitcast.13), channel_id=1, source_target_pairs={{0,32},{8,40},{16,48},{24,56},{32,64},{40,72},{48,80},{56,88},{64,... | collective-permute-start | bytes 786440 | tf_op jit(solution)/shard_map/gather_projections/ppermute | solution.py:358
  44.6 10.6 %collective-permute-start.2 = (bf16[4,128,256]{2,1,0:T(8,128)(2,1)S(1)}, bf16[4,128,256]{2,1,0:T(8,128)(2,1)S(1)}, u32[]{:S(2)}, u32[]{:S(2)}) collective-permute-start(bf16[4,128,256]{2,1,0:T(8,128)(2,1)S(1)} %bitcast.14), channel_id=1, source_target_pairs={{0,480},{8,488},{16,496},{24,504},{32,0},{40,8},{48,16},{56,24},{6... | collective-permute-start | bytes 786440 | tf_op jit(solution)/shard_map/gather_projections/ppermute | solution.py:358
  48.9 38.9 %collective-permute-start.6 = (bf16[16,128,128]{2,1,0:T(8,128)(2,1)}, bf16[16,128,128]{2,1,0:T(8,128)(2,1)}, u32[]{:S(2)}, u32[]{:S(2)}) collective-permute-start(bf16[16,128,128]{2,1,0:T(8,128)(2,1)} %pad_maximum_fusion), channel_id=1, source_target_pairs={{0,16},{8,24},{16,0},{24,8},{32,48},{40,56},{48,32},{56,40},{64,80... | collective-permute-start | bytes 1572872 | tf_op jit(solution)/shard_map/share_queries/ppermute | solution.py:375
  55.1 15.9 %copy-start.3 = (f32[128]{0:T(128)S(1)}, f32[128]{0:T(128)}, u32[]{:S(2)}) copy-start(f32[128]{0:T(128)} %param.11) | copy-start | bytes 1540
  55.1 42.1 %copy-start.2 = (s32[24]{0:T(128)S(1)}, s32[24]{0:T(128)}, u32[]{:S(2)}) copy-start(s32[24]{0:T(128)} %image_start_ref.3) | copy-start | bytes 292
  55.2 42.1 %copy-start.4 = (s32[128]{0:T(128)S(1)}, s32[128]{0:T(128)}, u32[]{:S(2)}) copy-start(s32[128]{0:T(128)} %slot_image_ref.1) | copy-start | bytes 1540
  56.2 7.4 %collective-permute-start.4 = (bf16[256,384]{1,0:T(8,128)(2,1)S(1)}, bf16[256,384]{1,0:T(8,128)(2,1)S(1)}, u32[]{:S(2)}, u32[]{:S(2)}) collective-permute-start(bf16[256,384]{1,0:T(8,128)(2,1)S(1)} %get-tuple-element.24), channel_id=1, source_target_pairs={{0,8},{8,0},{16,24},{24,16},{32,40},{40,32},{48,56},{56,48},{64,72... | collective-permute-start | bytes 589832 | tf_op jit(solution)/shard_map/sum_projections/ppermute | solution.py:375
  63.6 7.4 %collective-permute-start.5 = (bf16[128,384]{1,0:T(8,128)(2,1)S(1)}, bf16[128,384]{1,0:T(8,128)(2,1)S(1)}, u32[]{:S(2)}, u32[]{:S(2)}) collective-permute-start(bf16[128,384]{1,0:T(8,128)(2,1)S(1)} %sum_projections.2), channel_id=1, source_target_pairs={{0,16},{8,24},{16,0},{24,8},{32,48},{40,56},{48,32},{56,40},{64,80... | collective-permute-start | bytes 294920 | tf_op jit(solution)/shard_map/sum_projections/ppermute | solution.py:375
  87.8 14.9 %collective-permute-start.7 = (bf16[4,128,256]{2,1,0:T(8,128)(2,1)S(1)}, bf16[4,128,256]{2,1,0:T(8,128)(2,1)S(1)}, u32[]{:S(2)}, u32[]{:S(2)}) collective-permute-start(bf16[4,128,256]{2,1,0:T(8,128)(2,1)S(1)} %bitcast.16), channel_id=1, source_target_pairs={{0,64},{8,456},{16,80},{24,472},{32,96},{40,488},{48,112},{56,504}... | collective-permute-start | bytes 786440 | tf_op jit(solution)/shard_map/gather_keys_values/ppermute | solution.py:358
  90.8 13.4 %collective-permute-start.8 = (bf16[4,128,256]{2,1,0:T(8,128)(2,1)S(1)}, bf16[4,128,256]{2,1,0:T(8,128)(2,1)S(1)}, u32[]{:S(2)}, u32[]{:S(2)}) collective-permute-start(bf16[4,128,256]{2,1,0:T(8,128)(2,1)S(1)} %bitcast.17), channel_id=1, source_target_pairs={{0,32},{8,40},{16,48},{24,56},{32,64},{40,72},{48,80},{56,88},{64,... | collective-permute-start | bytes 786440 | tf_op jit(solution)/shard_map/gather_keys_values/ppermute | solution.py:358
  93.0 11.2 %collective-permute-start.9 = (bf16[4,128,256]{2,1,0:T(8,128)(2,1)S(1)}, bf16[4,128,256]{2,1,0:T(8,128)(2,1)S(1)}, u32[]{:S(2)}, u32[]{:S(2)}) collective-permute-start(bf16[4,128,256]{2,1,0:T(8,128)(2,1)S(1)} %bitcast.18), channel_id=1, source_target_pairs={{0,480},{8,488},{16,496},{24,504},{32,0},{40,8},{48,16},{56,24},{6... | collective-permute-start | bytes 786440 | tf_op jit(solution)/shard_map/gather_keys_values/ppermute | solution.py:358
  107.0 7.5 %collective-permute-start.10 = (bf16[256,1152]{1,0:T(8,128)(2,1)S(1)}, bf16[256,1152]{1,0:T(8,128)(2,1)S(1)}, u32[]{:S(2)}, u32[]{:S(2)}) collective-permute-start(bf16[256,1152]{1,0:T(8,128)(2,1)S(1)} %get-tuple-element.34), channel_id=1, source_target_pairs={{0,8},{8,0},{16,24},{24,16},{32,40},{40,32},{48,56},{56,48},{64,72... | collective-permute-start | bytes 1769480 | tf_op jit(solution)/shard_map/sum_attention/ppermute | solution.py:375
  114.8 11.6 %collective-permute-start.11 = (bf16[128,1152]{1,0:T(8,128)(2,1)S(1)}, bf16[128,1152]{1,0:T(8,128)(2,1)S(1)}, u32[]{:S(2)}, u32[]{:S(2)}) collective-permute-start(bf16[128,1152]{1,0:T(8,128)(2,1)S(1)} %sum_attention.3), channel_id=1, source_target_pairs={{0,16},{8,24},{16,0},{24,8},{32,48},{40,56},{48,32},{56,40},{64,80... | collective-permute-start | bytes 884744 | tf_op jit(solution)/shard_map/sum_attention/ppermute | solution.py:375

commit v3 on v2

--- a/solution.py
+++ b/solution.py
@@ -299,7 +299,7 @@
                 heads // together,
                 functools.partial(some_heads, packed=turn * group),
                 0,
-                unroll=2,
+                unroll=2 if pack else 1,
             )
 
     @pl.when(turns == 0)
@@ -325,7 +325,9 @@
     out_ref[:, cut:] = split_sums(join_sums(sums, heads), heads).astype(out_ref.dtype)
 
 
-def combine_kernel(image_start_ref, place_ref, gate_ref, kept_ref, core_ref, chip_ref, out_ref):
+def combine_kernel(
+    image_start_ref, place_ref, gate_ref, kept_ref, core_ref, chip_ref, out_ref, done_ref, sems
+):
     own, out_width = out_ref.shape
     width = kept_ref.shape[1]
     head_dim = width - out_width
@@ -344,9 +346,21 @@
 
     sums = join_sums(total(slice(out_width, width)), heads)
     share = jnp.where(seen, factor / jnp.where(seen, sums, 1.0), 0.0)
+    copies = []
+    step = 2
     for head in range(heads):
         columns = slice(head * head_dim, (head + 1) * head_dim)
-        out_ref[:, columns] = (total(columns) * share[:, head : head + 1]).astype(out_ref.dtype)
+        done_ref[:, columns] = (total(columns) * share[:, head : head + 1]).astype(done_ref.dtype)
+        if head % step == step - 1:
+            several = slice((head + 1 - step) * head_dim, (head + 1) * head_dim)
+            copies.append(
+                pltpu.make_async_copy(
+                    done_ref.at[:, several], out_ref.at[:, several], sems.at[head // step]
+                )
+            )
+            copies[-1].start()
+    for copy in copies:
+        copy.wait()
 
 
 def gather_along_z(block, beside=None):
@@ -571,7 +585,11 @@
             combine_kernel,
             out_shape=jax.ShapeDtypeStruct((tokens, q_cols), jnp.bfloat16),
             in_specs=[smem(), smem()] + [vmem()] * 4,
-            out_specs=vmem(),
+            out_specs=pl.BlockSpec(memory_space=pltpu.HBM),
+            scratch_shapes=[
+                pltpu.VMEM((tokens, q_cols), jnp.bfloat16),
+                pltpu.SemaphoreType.DMA((heads // 2,)),
+            ],
             compiler_params=params(),
         )(image_start, place, attn_gate.reshape(1, 1), kept, from_core, from_chip)
 

time: 129 us -> 129 us (level)
  starting transfers between devices: 56.3 us -> 54.9 us
    ppermute x6, starting transfers between devices: 26.6 us -> 25.1 us  [other_member(): return lax.ppermute(value, 'ctx', [(i, i ^ mask) for i in range(ctx_size)])]
  transfers between devices with their start and end apart: 13 -> 13, of which waited for: 5 -> 5; matrix products, arithmetic and copies ran while one was open for 1% -> 1% of each run, Pallas kernels for 7% -> 8%
where the time goes in v3:
time: 129 us; the launch traced here: 128 us
  starting transfers between devices  54.9 us (43%)
  blocking collectives  39.5 us (31%)
  Pallas kernels  16.7 us (13%)
  waiting for transfers between devices  14.9 us (12%)
    all_gather x2, blocking collectives, gather_along_z(): own = lax.all_gather(block, 'ctx', axis_index_groups=groups)  39.5 us
    ppermute x6, starting transfers between devices, other_member(): return lax.ppermute(value, 'ctx', [(i, i ^ mask) for i in range(ctx_size)])  25.1 us
    ppermute x6, starting transfers between devices, shift(): lax.ppermute(value, 'ctx', [(i, (i + moves[i]) % ctx_size) for i in range...  19 us
    ppermute x6, waiting for transfers between devices, other_member(): return lax.ppermute(value, 'ctx', [(i, i ^ mask) for i in range(ctx_size)])  13.5 us
    all_to_all x1, starting transfers between devices, local(): lax.all_to_all(mine, ('ctx', 'head'), 0, 0, axis_index_groups=whole_plane)  10.7 us
    pallas_call x1, Pallas kernels, local(): pl.pallas_call(functools.partial(attend_first_kernel, scale=scale, slots_...  5.44 us
    pallas_call x2, Pallas kernels, attend_last(): pl.pallas_call(functools.partial(attend_last_kernel, scale=scale, group=g...  4.37 us
  transfers between devices with their start and end apart: 13, of which 5 were waited for; matrix products, arithmetic and copies ran while one was open for 1% of the time, Pallas kernels for 8%

profile of v3, /device:TPU:1, one launch (start us, length us, event | category | flops | bytes accessed | tf_op | source)
XLA Modules:
  0.0 128.1 jit_solution(10478440638951056376)
XLA Ops:
  0.0 2.4 %spread_vision.1 = bf16[4,8,2,128,128]{4,3,2,1,0:T(8,128)(2,1)} custom-call(bf16[128,1024]{1,0:T(8,128)(2,1)} %x_ref.1), custom_call_target="tpu_custom_call" | custom-call | tf_op jit(solution)/shard_map/spread_vision/pallas_call | solution.py:431
  2.4 0.0 copy-start
  2.4 0.0 copy-start.1
  2.4 0.0 copy-start.5
  2.4 0.0 copy-start.6
  2.4 10.7 %all-to-all-start = ((bf16[32,2,128,128]{3,2,1,0:T(8,128)(2,1)}), bf16[32,2,128,128]{3,2,1,0:T(8,128)(2,1)S(1)}, u32[]{:S(2)}, u32[]{:S(2)}) async-start(bf16[32,2,128,128]{3,2,1,0:T(8,128)(2,1)} %bitcast.22), calls=%async_computation | async-start | bytes 4194304 | tf_op jit(solution)/shard_map/spread_vision/all_to_all | solution.py:445
  13.2 0.0 copy-done
  13.2 0.2 norm_queries.1.refs_1_
  13.4 2.2 %collective-permute-start = (bf16[8,128,128]{2,1,0:T(8,128)(2,1)S(1)}, bf16[8,128,128]{2,1,0:T(8,128)(2,1)S(1)}, u32[]{:S(2)}, u32[]{:S(2)}) collective-permute-start(bf16[8,128,128]{2,1,0:T(8,128)(2,1)S(1)} %norm_queries.1.refs_1_), channel_id=1, source_target_pairs={{0,8},{8,0},{16,24},{24,16},{32,40},{40,32},{48,56},{56,48},{64,72... | collective-permute-start | bytes 786440 | tf_op jit(solution)/shard_map/share_queries/ppermute | solution.py:389
  15.7 22.8 %all-gather = bf16[512,256]{1,0:T(8,128)(2,1)S(1)} all-gather(bf16[128,256]{1,0:T(8,128)(2,1)S(1)} %pad_maximum_fusion.1), channel_id=2, replica_groups={{0,128,256,384},{32,160,288,416},{64,192,320,448},{96,224,352,480},{8,1..., dimensions={0}, use_global_device_ids=true | all-gather | bytes 327680 | tf_op jit(solution)/shard_map/gather_projections/all_gather | solution.py:381
  38.5 3.1 %collective-permute-start.3 = (bf16[4,128,256]{2,1,0:T(8,128)(2,1)S(1)}, bf16[4,128,256]{2,1,0:T(8,128)(2,1)}, u32[]{:S(2)}, u32[]{:S(2)}) collective-permute-start(bf16[4,128,256]{2,1,0:T(8,128)(2,1)S(1)} %bitcast.12), channel_id=1, source_target_pairs={{0,64},{8,456},{16,80},{24,472},{32,96},{40,488},{48,112},{56,504}... | collective-permute-start | bytes 786440 | tf_op jit(solution)/shard_map/gather_projections/ppermute | solution.py:372
  41.6 3.0 %collective-permute-start.1 = (bf16[4,128,256]{2,1,0:T(8,128)(2,1)S(1)}, bf16[4,128,256]{2,1,0:T(8,128)(2,1)S(1)}, u32[]{:S(2)}, u32[]{:S(2)}) collective-permute-start(bf16[4,128,256]{2,1,0:T(8,128)(2,1)S(1)} %bitcast.13), channel_id=1, source_target_pairs={{0,32},{8,40},{16,48},{24,56},{32,64},{40,72},{48,80},{56,88},{64,... | collective-permute-start | bytes 786440 | tf_op jit(solution)/shard_map/gather_projections/ppermute | solution.py:372
  44.6 3.5 %collective-permute-start.2 = (bf16[4,128,256]{2,1,0:T(8,128)(2,1)S(1)}, bf16[4,128,256]{2,1,0:T(8,128)(2,1)S(1)}, u32[]{:S(2)}, u32[]{:S(2)}) collective-permute-start(bf16[4,128,256]{2,1,0:T(8,128)(2,1)S(1)} %bitcast.14), channel_id=1, source_target_pairs={{0,480},{8,488},{16,496},{24,504},{32,0},{40,8},{48,16},{56,24},{6... | collective-permute-start | bytes 786440 | tf_op jit(solution)/shard_map/gather_projections/ppermute | solution.py:372
  48.1 0.0 collective-permute-done.refs_3_
  48.1 0.0 all-to-all-done
  48.1 0.8 pad_maximum_fusion
  48.9 4.7 %collective-permute-start.6 = (bf16[16,128,128]{2,1,0:T(8,128)(2,1)}, bf16[16,128,128]{2,1,0:T(8,128)(2,1)}, u32[]{:S(2)}, u32[]{:S(2)}) collective-permute-start(bf16[16,128,128]{2,1,0:T(8,128)(2,1)} %pad_maximum_fusion), channel_id=1, source_target_pairs={{0,16},{8,24},{16,0},{24,8},{32,48},{40,56},{48,32},{56,40},{64,80... | collective-permute-start | bytes 1572872 | tf_op jit(solution)/shard_map/share_queries/ppermute | solution.py:389
  53.7 0.1 pad_add_fusion.place_ref
  53.7 0.0 collective-permute-done.3.refs_1_
  53.7 1.4 %project.2.refs_2_ = f32[512,256]{1,0:T(8,128)S(1)} custom-call(s32[2]{0:T(128)S(1)} %pad_add_fusion.place_ref, bf16[4,16,128,128]{3,2,1,0:T(8,128)(2,1)S(1)} %bitcast.10, bf16[4,128,256]{2,1,0:T(8,128)(2,1)S(1)} %bitcast.15, bf16[4,128,256]{2,1,0:T(8,128)(2,1)} %collective-permute-done.3.refs_1_), custom_call_target="tpu_custom_call" | custom-call | tf_op jit(solution)/shard_map/project/pallas_call | solution.py:459
  55.1 0.0 copy-start.3
  55.1 0.0 copy-start.2
  55.2 0.0 copy-start.4
  55.2 0.0 collective-permute-done.1.refs_0_
  55.2 0.0 collective-permute-done.2.refs_1_
  55.2 1.0 project.3
  56.2 6.3 %collective-permute-start.4 = (bf16[256,384]{1,0:T(8,128)(2,1)S(1)}, bf16[256,384]{1,0:T(8,128)(2,1)S(1)}, u32[]{:S(2)}, u32[]{:S(2)}) collective-permute-start(bf16[256,384]{1,0:T(8,128)(2,1)S(1)} %get-tuple-element.24), channel_id=1, source_target_pairs={{0,8},{8,0},{16,24},{24,16},{32,40},{40,32},{48,56},{56,48},{64,72... | collective-permute-start | bytes 589832 | tf_op jit(solution)/shard_map/sum_projections/ppermute | solution.py:389
  62.5 1.0 collective-permute-done.4.came_ref.core_ref
  63.6 4.1 %collective-permute-start.5 = (bf16[128,384]{1,0:T(8,128)(2,1)S(1)}, bf16[128,384]{1,0:T(8,128)(2,1)S(1)}, u32[]{:S(2)}, u32[]{:S(2)}) collective-permute-start(bf16[128,384]{1,0:T(8,128)(2,1)S(1)} %sum_projections.2), channel_id=1, source_target_pairs={{0,16},{8,24},{16,0},{24,8},{32,48},{40,56},{48,32},{56,40},{64,80... | collective-permute-start | bytes 294920 | tf_op jit(solution)/shard_map/sum_projections/ppermute | solution.py:389
  67.7 3.3 %collective-permute-done.5.chip_ref = bf16[128,384]{1,0:T(8,128)(2,1)S(1)} collective-permute-done((bf16[128,384]{1,0:T(8,128)(2,1)S(1)}, bf16[128,384]{1,0:T(8,128)(2,1)S(1)}, u32[]{:S(2)}, u32[]{:S(2)}) %collective-permute-start.5) | collective-permute-done | bytes 98336 | tf_op jit(solution)/shard_map/sum_projections/ppermute | solution.py:389
  71.0 0.1 sum_projections.3
  71.1 16.7 %all-gather.1 = bf16[512,256]{1,0:T(8,128)(2,1)S(1)} all-gather(bf16[128,256]{1,0:T(8,128)(2,1)S(1)} %sum_projections.3), channel_id=3, replica_groups={{0,128,256,384},{32,160,288,416},{64,192,320,448},{96,224,352,480},{8,1..., dimensions={0}, use_global_device_ids=true | all-gather | bytes 327680 | tf_op jit(solution)/shard_map/gather_keys_values/all_gather | solution.py:381
  87.8 0.0 collective-permute-done.6.refs_2_.refs_4_
  87.8 2.9 %collective-permute-start.7 = (bf16[4,128,256]{2,1,0:T(8,128)(2,1)S(1)}, bf16[4,128,256]{2,1,0:T(8,128)(2,1)S(1)}, u32[]{:S(2)}, u32[]{:S(2)}) collective-permute-start(bf16[4,128,256]{2,1,0:T(8,128)(2,1)S(1)} %bitcast.16), channel_id=1, source_target_pairs={{0,64},{8,456},{16,80},{24,472},{32,96},{40,488},{48,112},{56,504}... | collective-permute-start | bytes 786440 | tf_op jit(solution)/shard_map/gather_keys_values/ppermute | solution.py:372
  90.8 2.3 %collective-permute-start.8 = (bf16[4,128,256]{2,1,0:T(8,128)(2,1)S(1)}, bf16[4,128,256]{2,1,0:T(8,128)(2,1)S(1)}, u32[]{:S(2)}, u32[]{:S(2)}) collective-permute-start(bf16[4,128,256]{2,1,0:T(8,128)(2,1)S(1)} %bitcast.17), channel_id=1, source_target_pairs={{0,32},{8,40},{16,48},{24,56},{32,64},{40,72},{48,80},{56,88},{64,... | collective-permute-start | bytes 786440 | tf_op jit(solution)/shard_map/gather_keys_values/ppermute | solution.py:372
  93.0 4.2 %collective-permute-start.9 = (bf16[4,128,256]{2,1,0:T(8,128)(2,1)S(1)}, bf16[4,128,256]{2,1,0:T(8,128)(2,1)S(1)}, u32[]{:S(2)}, u32[]{:S(2)}) collective-permute-start(bf16[4,128,256]{2,1,0:T(8,128)(2,1)S(1)} %bitcast.18), channel_id=1, source_target_pairs={{0,480},{8,488},{16,496},{24,504},{32,0},{40,8},{48,16},{56,24},{6... | collective-permute-start | bytes 786440 | tf_op jit(solution)/shard_map/gather_keys_values/ppermute | solution.py:372
  97.3 5.4 %attend.2 = (bf16[512,1024]{1,0:T(8,128)(2,1)S(1)}, f32[512,128]{1,0:T(8,128)S(1)}, bf16[8,512,256]{2,1,0:T(8,128)(2,1)S(1)}, s32[49]{0:T(128)S(1)}) custom-call(s32[24]{0:T(128)S(1)} %copy-done.2, s32[128]{0:T(128)S(1)} %copy-done.4, s32[2]{0:T(128)S(1)} %pad_add_fusion.place_ref, bf16[4,128,256]{2,1,0:T(8,128)(2,1)S(1)} %bitcast.19, ...), custom_call_target="tpu_custom_call" | custom-call | flops 2147483648 | bytes 2359296 | tf_op jit(solution)/shard_map/attend/pallas_call | solution.py:515
  102.7 0.0 collective-permute-done.7.refs_3_
  102.7 1.5 %collective-permute-done.8.refs_4_ = bf16[4,128,256]{2,1,0:T(8,128)(2,1)S(1)} collective-permute-done((bf16[4,128,256]{2,1,0:T(8,128)(2,1)S(1)}, bf16[4,128,256]{2,1,0:T(8,128)(2,1)S(1)}, u32[]{:S(2)}, u32[]{:S(2)}) %collective-permute-start.8) | collective-permute-done | bytes 262176 | tf_op jit(solution)/shard_map/gather_keys_values/ppermute | solution.py:372
  104.2 0.0 collective-permute-done.9.refs_5_
  104.2 2.8 %attend.3 = (bf16[128,1152]{1,0:T(8,128)(2,1)S(1)}, bf16[256,1152]{1,0:T(8,128)(2,1)S(1)}, bf16[24,64,256]{2,1,0:T(8,128)(2,1)S(1)}, bf16[24,64,256]{2,1,0:T(8,128)(2,1)S(1)}) custom-call(s32[49]{0:T(128)S(1)} %get-tuple-element.29.plan_ref, bf16[512,1024]{1,0:T(8,128)(2,1)S(1)} %get-tuple-element.30.refs_0_, f32[512,128]{1,0:T(8,128)S(1)} %get-tuple-element.31.refs_1_, ...), custom_call_target="tpu_custom_call" | custom-call | flops 4831838208 | bytes 1769472 | tf_op jit(solution)/shard_map/attend/pallas_call | solution.py:545
  107.0 5.9 %collective-permute-start.10 = (bf16[256,1152]{1,0:T(8,128)(2,1)S(1)}, bf16[256,1152]{1,0:T(8,128)(2,1)S(1)}, u32[]{:S(2)}, u32[]{:S(2)}) collective-permute-start(bf16[256,1152]{1,0:T(8,128)(2,1)S(1)} %get-tuple-element.34), channel_id=1, source_target_pairs={{0,8},{8,0},{16,24},{24,16},{32,40},{40,32},{48,56},{56,48},{64,72... | collective-permute-start | bytes 1769480 | tf_op jit(solution)/shard_map/sum_attention/ppermute | solution.py:389
  112.9 1.6 %collective-permute-done.10.came_ref.core_ref = bf16[256,1152]{1,0:T(8,128)(2,1)S(1)} collective-permute-done((bf16[256,1152]{1,0:T(8,128)(2,1)S(1)}, bf16[256,1152]{1,0:T(8,128)(2,1)S(1)}, u32[]{:S(2)}, u32[]{:S(2)}) %collective-permute-start.10) | collective-permute-done | bytes 589856 | tf_op jit(solution)/shard_map/sum_attention/ppermute | solution.py:389
  114.5 0.2 sum_attention.3
  114.8 1.9 %collective-permute-start.11 = (bf16[128,1152]{1,0:T(8,128)(2,1)S(1)}, bf16[128,1152]{1,0:T(8,128)(2,1)S(1)}, u32[]{:S(2)}, u32[]{:S(2)}) collective-permute-start(bf16[128,1152]{1,0:T(8,128)(2,1)S(1)} %sum_attention.3), channel_id=1, source_target_pairs={{0,16},{8,24},{16,0},{24,8},{32,48},{40,56},{48,32},{56,40},{64,80... | collective-permute-start | bytes 884744 | tf_op jit(solution)/shard_map/sum_attention/ppermute | solution.py:389
  117.3 1.6 %sum_attention.4.kept_ref = bf16[128,1152]{1,0:T(8,128)(2,1)S(1)} custom-call(s32[49]{0:T(128)S(1)} %get-tuple-element.29.plan_ref, bf16[512,1024]{1,0:T(8,128)(2,1)S(1)} %get-tuple-element.30.refs_0_, f32[512,128]{1,0:T(8,128)S(1)} %get-tuple-element.31.refs_1_, bf16[8,512,256]{2,1,0:T(8,128)(2,1)S(1)} %get-tuple-element.32.refs_2_, ...), custom_call_target="tpu_custom_call" | custom-call | flops 1610612736 | bytes 589824 | tf_op jit(solution)/shard_map/sum_attention/pallas_call | solution.py:545
  118.9 7.5 %collective-permute-done.11.chip_ref = bf16[128,1152]{1,0:T(8,128)(2,1)S(1)} collective-permute-done((bf16[128,1152]{1,0:T(8,128)(2,1)S(1)}, bf16[128,1152]{1,0:T(8,128)(2,1)S(1)}, u32[]{:S(2)}, u32[]{:S(2)}) %collective-permute-start.11) | collective-permute-done | bytes 294944 | tf_op jit(solution)/shard_map/sum_attention/ppermute | solution.py:389
  126.4 1.5 %sum_attention.5 = bf16[128,1024]{1,0:T(8,128)(2,1)} custom-call(s32[24]{0:T(128)S(1)} %copy-done.2, s32[2]{0:T(128)S(1)} %pad_add_fusion.place_ref, f32[1,1]{1,0:T(1,128)} %bitcast.9.gate_ref, bf16[128,1152]{1,0:T(8,128)(2,1)S(1)} %sum_attention.4.kept_ref, bf16[256,1152]{1,0:T(8,128)(2,1)S(1)} %collective-permute-done.10.came_ref.core_ref, ...), custom_call_target="tpu_custom_call" | custom-call | tf_op jit(solution)/shard_map/sum_attention/pallas_call | solution.py:584
  (8 shorter events, 0.1 us)
Async XLA Ops:
  2.4 10.8 %copy-start = (bf16[128,1024]{1,0:T(8,128)(2,1)S(1)}, bf16[128,1024]{1,0:T(8,128)(2,1)}, u32[]{:S(2)}) copy-start(bf16[128,1024]{1,0:T(8,128)(2,1)} %q_ref.1) | copy-start | bytes 786436
  2.4 10.8 %copy-start.1 = (f32[128]{0:T(128)S(1)}, f32[128]{0:T(128)}, u32[]{:S(2)}) copy-start(f32[128]{0:T(128)} %param.10) | copy-start | bytes 1540
  2.4 13.2 %copy-start.5 = (bf16[128,128]{1,0:T(8,128)(2,1)S(1)}, bf16[128,128]{1,0:T(8,128)(2,1)}, u32[]{:S(2)}) copy-start(bf16[128,128]{1,0:T(8,128)(2,1)} %param.15) | copy-start | bytes 98308
  2.4 13.2 %copy-start.6 = (bf16[128,128]{1,0:T(8,128)(2,1)S(1)}, bf16[128,128]{1,0:T(8,128)(2,1)}, u32[]{:S(2)}) copy-start(bf16[128,128]{1,0:T(8,128)(2,1)} %param.14) | copy-start | bytes 98308
  2.4 45.7 %all-to-all-start = ((bf16[32,2,128,128]{3,2,1,0:T(8,128)(2,1)}), bf16[32,2,128,128]{3,2,1,0:T(8,128)(2,1)S(1)}, u32[]{:S(2)}, u32[]{:S(2)}) async-start(bf16[32,2,128,128]{3,2,1,0:T(8,128)(2,1)} %bitcast.22), calls=%async_computation | async-start | bytes 4194304 | tf_op jit(solution)/shard_map/spread_vision/all_to_all | solution.py:445
  13.4 34.7 %collective-permute-start = (bf16[8,128,128]{2,1,0:T(8,128)(2,1)S(1)}, bf16[8,128,128]{2,1,0:T(8,128)(2,1)S(1)}, u32[]{:S(2)}, u32[]{:S(2)}) collective-permute-start(bf16[8,128,128]{2,1,0:T(8,128)(2,1)S(1)} %norm_queries.1.refs_1_), channel_id=1, source_target_pairs={{0,8},{8,0},{16,24},{24,16},{32,40},{40,32},{48,56},{56,48},{64,72... | collective-permute-start | bytes 786440 | tf_op jit(solution)/shard_map/share_queries/ppermute | solution.py:389
  38.5 15.3 %collective-permute-start.3 = (bf16[4,128,256]{2,1,0:T(8,128)(2,1)S(1)}, bf16[4,128,256]{2,1,0:T(8,128)(2,1)}, u32[]{:S(2)}, u32[]{:S(2)}) collective-permute-start(bf16[4,128,256]{2,1,0:T(8,128)(2,1)S(1)} %bitcast.12), channel_id=1, source_target_pairs={{0,64},{8,456},{16,80},{24,472},{32,96},{40,488},{48,112},{56,504}... | collective-permute-start | bytes 786440 | tf_op jit(solution)/shard_map/gather_projections/ppermute | solution.py:372
  41.6 13.6 %collective-permute-start.1 = (bf16[4,128,256]{2,1,0:T(8,128)(2,1)S(1)}, bf16[4,128,256]{2,1,0:T(8,128)(2,1)S(1)}, u32[]{:S(2)}, u32[]{:S(2)}) collective-permute-start(bf16[4,128,256]{2,1,0:T(8,128)(2,1)S(1)} %bitcast.13), channel_id=1, source_target_pairs={{0,32},{8,40},{16,48},{24,56},{32,64},{40,72},{48,80},{56,88},{64,... | collective-permute-start | bytes 786440 | tf_op jit(solution)/shard_map/gather_projections/ppermute | solution.py:372
  44.6 10.6 %collective-permute-start.2 = (bf16[4,128,256]{2,1,0:T(8,128)(2,1)S(1)}, bf16[4,128,256]{2,1,0:T(8,128)(2,1)S(1)}, u32[]{:S(2)}, u32[]{:S(2)}) collective-permute-start(bf16[4,128,256]{2,1,0:T(8,128)(2,1)S(1)} %bitcast.14), channel_id=1, source_target_pairs={{0,480},{8,488},{16,496},{24,504},{32,0},{40,8},{48,16},{56,24},{6... | collective-permute-start | bytes 786440 | tf_op jit(solution)/shard_map/gather_projections/ppermute | solution.py:372
  48.9 38.9 %collective-permute-start.6 = (bf16[16,128,128]{2,1,0:T(8,128)(2,1)}, bf16[16,128,128]{2,1,0:T(8,128)(2,1)}, u32[]{:S(2)}, u32[]{:S(2)}) collective-permute-start(bf16[16,128,128]{2,1,0:T(8,128)(2,1)} %pad_maximum_fusion), channel_id=1, source_target_pairs={{0,16},{8,24},{16,0},{24,8},{32,48},{40,56},{48,32},{56,40},{64,80... | collective-permute-start | bytes 1572872 | tf_op jit(solution)/shard_map/share_queries/ppermute | solution.py:389
  55.1 15.9 %copy-start.3 = (f32[128]{0:T(128)S(1)}, f32[128]{0:T(128)}, u32[]{:S(2)}) copy-start(f32[128]{0:T(128)} %param.11) | copy-start | bytes 1540
  55.1 42.1 %copy-start.2 = (s32[24]{0:T(128)S(1)}, s32[24]{0:T(128)}, u32[]{:S(2)}) copy-start(s32[24]{0:T(128)} %image_start_ref.3) | copy-start | bytes 292
  55.2 42.1 %copy-start.4 = (s32[128]{0:T(128)S(1)}, s32[128]{0:T(128)}, u32[]{:S(2)}) copy-start(s32[128]{0:T(128)} %slot_image_ref.1) | copy-start | bytes 1540
  56.2 7.4 %collective-permute-start.4 = (bf16[256,384]{1,0:T(8,128)(2,1)S(1)}, bf16[256,384]{1,0:T(8,128)(2,1)S(1)}, u32[]{:S(2)}, u32[]{:S(2)}) collective-permute-start(bf16[256,384]{1,0:T(8,128)(2,1)S(1)} %get-tuple-element.24), channel_id=1, source_target_pairs={{0,8},{8,0},{16,24},{24,16},{32,40},{40,32},{48,56},{56,48},{64,72... | collective-permute-start | bytes 589832 | tf_op jit(solution)/shard_map/sum_projections/ppermute | solution.py:389
  63.6 7.4 %collective-permute-start.5 = (bf16[128,384]{1,0:T(8,128)(2,1)S(1)}, bf16[128,384]{1,0:T(8,128)(2,1)S(1)}, u32[]{:S(2)}, u32[]{:S(2)}) collective-permute-start(bf16[128,384]{1,0:T(8,128)(2,1)S(1)} %sum_projections.2), channel_id=1, source_target_pairs={{0,16},{8,24},{16,0},{24,8},{32,48},{40,56},{48,32},{56,40},{64,80... | collective-permute-start | bytes 294920 | tf_op jit(solution)/shard_map/sum_projections/ppermute | solution.py:389
  87.8 14.9 %collective-permute-start.7 = (bf16[4,128,256]{2,1,0:T(8,128)(2,1)S(1)}, bf16[4,128,256]{2,1,0:T(8,128)(2,1)S(1)}, u32[]{:S(2)}, u32[]{:S(2)}) collective-permute-start(bf16[4,128,256]{2,1,0:T(8,128)(2,1)S(1)} %bitcast.16), channel_id=1, source_target_pairs={{0,64},{8,456},{16,80},{24,472},{32,96},{40,488},{48,112},{56,504}... | collective-permute-start | bytes 786440 | tf_op jit(solution)/shard_map/gather_keys_values/ppermute | solution.py:372
  90.8 13.4 %collective-permute-start.8 = (bf16[4,128,256]{2,1,0:T(8,128)(2,1)S(1)}, bf16[4,128,256]{2,1,0:T(8,128)(2,1)S(1)}, u32[]{:S(2)}, u32[]{:S(2)}) collective-permute-start(bf16[4,128,256]{2,1,0:T(8,128)(2,1)S(1)} %bitcast.17), channel_id=1, source_target_pairs={{0,32},{8,40},{16,48},{24,56},{32,64},{40,72},{48,80},{56,88},{64,... | collective-permute-start | bytes 786440 | tf_op jit(solution)/shard_map/gather_keys_values/ppermute | solution.py:372
  93.0 11.2 %collective-permute-start.9 = (bf16[4,128,256]{2,1,0:T(8,128)(2,1)S(1)}, bf16[4,128,256]{2,1,0:T(8,128)(2,1)S(1)}, u32[]{:S(2)}, u32[]{:S(2)}) collective-permute-start(bf16[4,128,256]{2,1,0:T(8,128)(2,1)S(1)} %bitcast.18), channel_id=1, source_target_pairs={{0,480},{8,488},{16,496},{24,504},{32,0},{40,8},{48,16},{56,24},{6... | collective-permute-start | bytes 786440 | tf_op jit(solution)/shard_map/gather_keys_values/ppermute | solution.py:372
  107.0 7.5 %collective-permute-start.10 = (bf16[256,1152]{1,0:T(8,128)(2,1)S(1)}, bf16[256,1152]{1,0:T(8,128)(2,1)S(1)}, u32[]{:S(2)}, u32[]{:S(2)}) collective-permute-start(bf16[256,1152]{1,0:T(8,128)(2,1)S(1)} %get-tuple-element.34), channel_id=1, source_target_pairs={{0,8},{8,0},{16,24},{24,16},{32,40},{40,32},{48,56},{56,48},{64,72... | collective-permute-start | bytes 1769480 | tf_op jit(solution)/shard_map/sum_attention/ppermute | solution.py:389
  114.8 11.6 %collective-permute-start.11 = (bf16[128,1152]{1,0:T(8,128)(2,1)S(1)}, bf16[128,1152]{1,0:T(8,128)(2,1)S(1)}, u32[]{:S(2)}, u32[]{:S(2)}) collective-permute-start(bf16[128,1152]{1,0:T(8,128)(2,1)S(1)} %sum_attention.3), channel_id=1, source_target_pairs={{0,16},{8,24},{16,0},{24,8},{32,48},{40,56},{48,32},{56,40},{64,80... | collective-permute-start | bytes 884744 | tf_op jit(solution)/shard_map/sum_attention/ppermute | solution.py:389
